TPU v7x, 32 devices: a whole 2x2x4 slice. The times are simulated.
32 devices in a mesh: section: 4 (over y, x), wide: 8 (over z, core).
Axes of the slice: x: 2, y: 2, z: 4, core: 2. Of those that a mesh axis runs over, the one named last changes fastest.
Arguments:
- patches_in: bfloat16 [4, 6272, 384], P(None, 'wide'), may hold values from -6 to 6
- cotangent: bfloat16 [4, 6272, 384], P(None, 'wide'), may hold values from -6 to 6
- task_ids: int32 [4, 32], P(None, 'wide'), may hold values from 0 to 1
- routes: int32 [4, 6272, 2], P(None, 'wide'), may hold values from 0 to 3, as said below
- keep_mask: int32 [4, 6272, 2], P(None, 'wide'), may hold values from 0 to 1, as said below
- first_gain: float32 [384], replicated, may hold values from 0.5 to 1.5
- first_shift: float32 [384], replicated, may hold values from -1.25 to 1.25
- first_proj: bfloat16 [384, 1152], P('section'), may hold values from -0.3125 to 0.3125
- first_out: bfloat16 [384, 384], P('section'), may hold values from -1.75 to 1.75
- first_bias: float32 [384], replicated, may hold values from -1.25 to 1.25
- dense_gain: float32 [384], replicated, may hold values from 0.5 to 1.5
- dense_shift: float32 [384], replicated, may hold values from -1.25 to 1.25
- dense_up: bfloat16 [384, 1536], P('section'), may hold values from -0.3125 to 0.3125
- hidden_bias: float32 [1536], replicated, may hold values from -3 to 3
- dense_down: bfloat16 [1536, 384], P('section'), may hold values from -0.15625 to 0.15625
- dense_bias: float32 [384], replicated, may hold values from -1.25 to 1.25
- second_gain: float32 [384], replicated, may hold values from 0.5 to 1.5
- second_shift: float32 [384], replicated, may hold values from -1.25 to 1.25
- second_proj: bfloat16 [384, 1152], P('section'), may hold values from -0.3125 to 0.3125
- second_out: bfloat16 [384, 384], P('section'), may hold values from -1.75 to 1.75
- second_bias: float32 [384], replicated, may hold values from -1.25 to 1.25
- mixture_gain: float32 [384], replicated, may hold values from 0.5 to 1.5
- mixture_shift: float32 [384], replicated, may hold values from -1.25 to 1.25
- router: bfloat16 [384, 8], P('section'), may hold values from -0.21875 to 0.21875
- expert_up: bfloat16 [4, 384, 1536], P('section'), may hold values from -0.3125 to 0.3125
- expert_down: bfloat16 [4, 1536, 384], P('section'), may hold values from -0.3125 to 0.3125
Outputs:
- block_output: bfloat16 [4, 6272, 384], P('section', 'wide')
- input_grad: bfloat16 [4, 6272, 384], P('section', 'wide')
- grad_first_gain: float32 [384], P('section')
- grad_first_shift: float32 [384], P('section')
- grad_first_proj: float32 [384, 1152], P('section')
- grad_first_out: float32 [384, 384], P('section')
- grad_first_bias: float32 [384], P('section')
- grad_dense_gain: float32 [384], P('section')
- grad_dense_shift: float32 [384], P('section')
- grad_dense_up: float32 [384, 1536], P('section')
- grad_hidden_bias: float32 [1536], P('section')
- grad_dense_down: float32 [1536, 384], P('section')
- grad_dense_bias: float32 [384], P('section')
- grad_second_gain: float32 [384], P('section')
- grad_second_shift: float32 [384], P('section')
- grad_second_proj: float32 [384, 1152], P('section')
- grad_second_out: float32 [384, 384], P('section')
- grad_second_bias: float32 [384], P('section')
- grad_mixture_gain: float32 [384], P('section')
- grad_mixture_shift: float32 [384], P('section')
- grad_router: float32 [384, 8], P('section')
- grad_expert_up: float32 [4, 384, 1536], P('section')
- grad_expert_down: float32 [4, 1536, 384], P('section')
Inputs may be any that keep to these rules, and one draw needn't show every extreme that they name: `routes`: each row names 2 different experts. keep_mask[m, r, k] = 1 exactly when fewer than 488 earlier routes of the same micro-batch and the same 4 * 196 rows of one index of wide (earlier rows, or a smaller k of the same row) name the same expert; in each such block some expert has 488 kept routes.
All inputs are finite; a program needn't handle non-finite values.
Results may differ from a plain program's by a relative error of at most 0.02.
Values may be sent and summed in bfloat16 or wider, within the bound.
A program may use at most 320 MiB of HBM per device.

v0:
```python
import jax
import jax.numpy as jnp
from jax import lax
from jax.sharding import PartitionSpec as P

HEADS = 6
HEAD_DIM = 64
PATCHES = 196
EXPERTS = 4
TOPK = 2
TASKS = 2
CAPACITY = 488


EPSILON = 1e-06
HIGHEST = lax.Precision.HIGHEST
SECTION_GROUPS = ((0, 5), (5, 11), (11, 16), (16, 21))
MATRIX_GROUPS = ((2, 3), (7, 9), (13, 14), (18, 19, 20))
MATRIX_INDEX = (2, 3, 7, 9, 13, 14, 18, 19, 20)


def as_sent(shard):

    def short(part):
        return part.astype(jnp.bfloat16) if part.dtype == jnp.float32 else part

    return jax.tree.map(short, shard)


def passed_along(block, axis, distance):
    devices = range(lax.axis_size(axis))
    route = [(i - distance, i) for i in devices if i - distance in devices]
    return lax.ppermute(block, axis, route)


def layer_norm(residual, norm_gain, norm_shift):
    middle = jnp.mean(residual, axis=-1, keepdims=True)
    centered = residual - middle
    spread = jnp.mean(centered * centered, axis=-1, keepdims=True)
    return centered * lax.rsqrt(spread + EPSILON) * norm_gain + norm_shift


def gelu_exact(hidden):
    return jax.nn.gelu(hidden, approximate=False)


def inner_left(left, right):
    return lax.dot_general(
        left, right, (((0,), (0,)), ((), ())), preferred_element_type=jnp.float32
    )


def inner_right(left, right):
    return lax.dot_general(
        left, right, (((1,), (1,)), ((), ())), preferred_element_type=jnp.float32
    )


def attend_parts(normed, in_weight):
    length = normed.shape[0]
    images = length // PATCHES
    projected = jnp.dot(normed, in_weight, preferred_element_type=jnp.float32).astype(jnp.bfloat16)
    shaped = projected.reshape(images, PATCHES, 3, HEADS, HEAD_DIM)
    query_heads = shaped[:, :, 0]
    key_heads = shaped[:, :, 1]
    value_heads = shaped[:, :, 2]
    scores = jnp.einsum(
        "iqhd,ikhd->ihqk", query_heads, key_heads, preferred_element_type=jnp.float32
    )
    softened = jax.nn.softmax(scores * HEAD_DIM ** (-0.5), axis=-1)
    rounded = softened.astype(jnp.bfloat16)
    context = jnp.einsum(
        "ihqk,ikhd->iqhd", rounded, value_heads, preferred_element_type=jnp.float32
    )
    context = context.reshape(length, HEADS * HEAD_DIM).astype(jnp.bfloat16)
    return (query_heads, key_heads, value_heads, softened, rounded, context)


def attend_forward(incoming, norm_gain, norm_shift, in_weight, out_weight, out_bias):
    residual = incoming.astype(jnp.float32)
    normed = layer_norm(residual, norm_gain, norm_shift).astype(jnp.bfloat16)
    context = attend_parts(normed, in_weight)[5]
    branch = jnp.dot(context, out_weight, preferred_element_type=jnp.float32) + out_bias
    return (residual + branch).astype(jnp.bfloat16)


def attend_backward(incoming, upstream, norm_gain, norm_shift, in_weight, out_weight, out_bias):
    residual = incoming.astype(jnp.float32)
    normed, norm_pull = jax.vjp(layer_norm, residual, norm_gain, norm_shift)
    normed = normed.astype(jnp.bfloat16)
    query_heads, key_heads, value_heads, softened, rounded, context = attend_parts(
        normed, in_weight
    )
    upstream_f = upstream.astype(jnp.float32)
    grad_out = inner_left(context, upstream)
    grad_bias = jnp.sum(upstream_f, axis=0)
    grad_context = inner_right(upstream, out_weight).astype(jnp.bfloat16).reshape(query_heads.shape)
    grad_soft = jnp.einsum(
        "iqhd,ikhd->ihqk", grad_context, value_heads, preferred_element_type=jnp.float32
    )
    grad_values = jnp.einsum(
        "ihqk,iqhd->ikhd", rounded, grad_context, preferred_element_type=jnp.float32
    )
    grad_scores = softened * (grad_soft - jnp.sum(softened * grad_soft, axis=-1, keepdims=True))
    grad_scores = grad_scores.astype(jnp.bfloat16)
    scaling = HEAD_DIM ** (-0.5)
    grad_query = (
        jnp.einsum("ihqk,ikhd->iqhd", grad_scores, key_heads, preferred_element_type=jnp.float32)
        * scaling
    )
    grad_keys = (
        jnp.einsum("ihqk,iqhd->ikhd", grad_scores, query_heads, preferred_element_type=jnp.float32)
        * scaling
    )
    grad_mixed = jnp.stack([grad_query, grad_keys, grad_values], axis=2)
    grad_mixed = grad_mixed.reshape(residual.shape[0], 3 * HEADS * HEAD_DIM).astype(jnp.bfloat16)
    grad_proj = inner_left(normed, grad_mixed)
    grad_normed = inner_right(grad_mixed, in_weight)
    grad_input, grad_gain, grad_shift = norm_pull(grad_normed)
    passed = (upstream_f + grad_input).astype(jnp.bfloat16)
    return (passed, (grad_gain, grad_shift, grad_proj, grad_out, grad_bias))


def dense_forward(incoming, norm_gain, norm_shift, up_weight, up_bias, down_weight, down_bias):
    residual = incoming.astype(jnp.float32)
    normed = layer_norm(residual, norm_gain, norm_shift).astype(jnp.bfloat16)
    hidden = jnp.dot(normed, up_weight, preferred_element_type=jnp.float32) + up_bias
    active = gelu_exact(hidden).astype(jnp.bfloat16)
    branch = jnp.dot(active, down_weight, preferred_element_type=jnp.float32) + down_bias
    return (residual + branch).astype(jnp.bfloat16)


def dense_backward(
    incoming, upstream, norm_gain, norm_shift, up_weight, up_bias, down_weight, down_bias
):
    residual = incoming.astype(jnp.float32)
    normed, norm_pull = jax.vjp(layer_norm, residual, norm_gain, norm_shift)
    normed = normed.astype(jnp.bfloat16)
    hidden = jnp.dot(normed, up_weight, preferred_element_type=jnp.float32) + up_bias
    active, gelu_pull = jax.vjp(gelu_exact, hidden)
    active = active.astype(jnp.bfloat16)
    upstream_f = upstream.astype(jnp.float32)
    grad_down = inner_left(active, upstream)
    grad_down_bias = jnp.sum(upstream_f, axis=0)
    grad_hidden = gelu_pull(inner_right(upstream, down_weight))[0].astype(jnp.bfloat16)
    grad_up = inner_left(normed, grad_hidden)
    grad_up_bias = jnp.sum(grad_hidden.astype(jnp.float32), axis=0)
    grad_normed = inner_right(grad_hidden, up_weight)
    grad_input, grad_gain, grad_shift = norm_pull(grad_normed)
    passed = (upstream_f + grad_input).astype(jnp.bfloat16)
    return (passed, (grad_gain, grad_shift, grad_up, grad_up_bias, grad_down, grad_down_bias))


def mixture_slots(route_rows, keep_rows):
    length = route_rows.shape[0]
    expert_ids = jnp.arange(EXPERTS, dtype=jnp.int32)
    chosen = (route_rows[:, :, None] == expert_ids[None, None, :]) & (keep_rows[:, :, None] == 1)
    flat_hits = chosen.reshape(length * TOPK, EXPERTS).astype(jnp.int32)
    position = jnp.cumsum(flat_hits, axis=0) - 1
    slot_index = jnp.where(
        flat_hits == 1, expert_ids[None, :] * CAPACITY + position, EXPERTS * CAPACITY
    )
    source = jnp.broadcast_to(
        jnp.repeat(jnp.arange(length, dtype=jnp.int32), TOPK)[:, None], slot_index.shape
    )
    slot_owner = jnp.full((EXPERTS * CAPACITY,), length, jnp.int32)
    slot_owner = slot_owner.at[slot_index.reshape(-1)].set(source.reshape(-1), mode="drop")
    selected = jnp.sum(chosen.astype(jnp.float32), axis=1)
    return (slot_owner.reshape(EXPERTS, CAPACITY), selected)


def mixture_gates(logits_all, picked, selected):
    logits = jnp.einsum(
        "rt,rte->re", picked, logits_all.reshape(-1, TASKS, EXPERTS), precision=HIGHEST
    )
    return jax.nn.softmax(logits, axis=-1) * selected


def mixture_common(
    incoming, task_rows, route_rows, keep_rows, norm_gain, norm_shift, router, up_weight
):
    residual = incoming.astype(jnp.float32)
    normed, norm_pull = jax.vjp(layer_norm, residual, norm_gain, norm_shift)
    normed = normed.astype(jnp.bfloat16)
    picked = (task_rows[:, None] == jnp.arange(TASKS, dtype=jnp.int32)[None, :]).astype(jnp.float32)
    slot_owner, selected = mixture_slots(route_rows, keep_rows)
    logits_all = jnp.dot(normed, router, preferred_element_type=jnp.float32)

    def gates_only(logit_values):
        return mixture_gates(logit_values, picked, selected)

    combine, gates_pull = jax.vjp(gates_only, logits_all)
    padded = jnp.concatenate([normed, jnp.zeros((1, normed.shape[1]), jnp.bfloat16)], axis=0)
    inputs = padded[slot_owner]
    expert_ids = jnp.arange(EXPERTS, dtype=jnp.int32)
    combine_pad = jnp.concatenate([combine, jnp.zeros((1, EXPERTS), jnp.float32)], axis=0)
    slot_combine = combine_pad[slot_owner, expert_ids[:, None]]
    hidden = jnp.einsum("ecd,edf->ecf", inputs, up_weight, preferred_element_type=jnp.float32)
    return (residual, normed, norm_pull, slot_owner, gates_pull, inputs, slot_combine, hidden)


def mixture_forward(
    incoming,
    task_rows,
    route_rows,
    keep_rows,
    norm_gain,
    norm_shift,
    router,
    up_weight,
    down_weight,
):
    residual, normed, norm_pull, slot_owner, gates_pull, inputs, slot_combine, hidden = (
        mixture_common(
            incoming, task_rows, route_rows, keep_rows, norm_gain, norm_shift, router, up_weight
        )
    )
    length = residual.shape[0]
    active = gelu_exact(hidden).astype(jnp.bfloat16)
    result = jnp.einsum(
        "ecf,efd->ecd", active, down_weight, preferred_element_type=jnp.float32
    ).astype(jnp.bfloat16)
    weighted = (slot_combine[..., None] * result.astype(jnp.float32)).reshape(-1, residual.shape[1])
    branch = jax.ops.segment_sum(weighted, slot_owner.reshape(-1), num_segments=length + 1)[:length]
    return (residual + branch).astype(jnp.bfloat16)


def mixture_backward(
    incoming,
    upstream,
    task_rows,
    route_rows,
    keep_rows,
    norm_gain,
    norm_shift,
    router,
    up_weight,
    down_weight,
):
    residual, normed, norm_pull, slot_owner, gates_pull, inputs, slot_combine, hidden = (
        mixture_common(
            incoming, task_rows, route_rows, keep_rows, norm_gain, norm_shift, router, up_weight
        )
    )
    length = residual.shape[0]
    model_width = residual.shape[1]
    active, gelu_pull = jax.vjp(gelu_exact, hidden)
    active = active.astype(jnp.bfloat16)
    result = jnp.einsum(
        "ecf,efd->ecd", active, down_weight, preferred_element_type=jnp.float32
    ).astype(jnp.bfloat16)
    upstream_f = upstream.astype(jnp.float32)
    grad_slots = jnp.concatenate([upstream, jnp.zeros((1, model_width), jnp.bfloat16)], axis=0)[
        slot_owner
    ].astype(jnp.float32)
    grad_result = (slot_combine[..., None] * grad_slots).astype(jnp.bfloat16)
    grad_slot_combine = jnp.sum(grad_slots * result.astype(jnp.float32), axis=-1)
    expert_ids = jnp.arange(EXPERTS, dtype=jnp.int32)
    grad_combine = (
        jnp.zeros((length + 1, EXPERTS), jnp.float32)
        .at[slot_owner, expert_ids[:, None]]
        .add(grad_slot_combine)[:length]
    )
    grad_logits = gates_pull(grad_combine)[0].astype(jnp.bfloat16)
    grad_router = inner_left(normed, grad_logits)
    grad_normed = inner_right(grad_logits, router)
    grad_active = jnp.einsum(
        "ecd,efd->ecf", grad_result, down_weight, preferred_element_type=jnp.float32
    )
    grad_hidden = gelu_pull(grad_active)[0].astype(jnp.bfloat16)
    grad_down = jnp.einsum("ecf,ecd->efd", active, grad_result, preferred_element_type=jnp.float32)
    grad_up = jnp.einsum("ecd,ecf->edf", inputs, grad_hidden, preferred_element_type=jnp.float32)
    grad_inputs = jnp.einsum(
        "ecf,edf->ecd", grad_hidden, up_weight, preferred_element_type=jnp.float32
    )
    grad_normed = (
        grad_normed
        + jax.ops.segment_sum(
            grad_inputs.reshape(-1, model_width), slot_owner.reshape(-1), num_segments=length + 1
        )[:length]
    )
    grad_input, grad_gain, grad_shift = norm_pull(grad_normed)
    passed = (upstream_f + grad_input).astype(jnp.bfloat16)
    return (passed, (grad_gain, grad_shift, grad_router, grad_up, grad_down))


def add_into(totals, start, gradients):
    updated = list(totals)
    for offset, member in enumerate(gradients):
        updated[start + offset] = updated[start + offset] + member
    return tuple(updated)


def pack_group(totals, start, stop, parts_count, longest):
    pieces = [totals[member].reshape(parts_count, -1) for member in range(start, stop)]
    joined = jnp.concatenate(pieces, axis=1)
    return jnp.pad(joined, ((0, 0), (0, longest - joined.shape[1])))


def with_matrices(params, matrices):
    updated = list(params)
    for position, member in enumerate(MATRIX_INDEX):
        updated[member] = matrices[position]
    return tuple(updated)


def local(
    patches_in,
    cotangent,
    task_ids,
    routes,
    keep_mask,
    first_gain,
    first_shift,
    first_proj,
    first_out,
    first_bias,
    dense_gain,
    dense_shift,
    dense_up,
    hidden_bias,
    dense_down,
    dense_bias,
    second_gain,
    second_shift,
    second_proj,
    second_out,
    second_bias,
    mixture_gain,
    mixture_shift,
    router,
    expert_up,
    expert_down,
):
    shards = (
        first_gain,
        first_shift,
        first_proj,
        first_out,
        first_bias,
        dense_gain,
        dense_shift,
        dense_up,
        hidden_bias,
        dense_down,
        dense_bias,
        second_gain,
        second_shift,
        second_proj,
        second_out,
        second_bias,
        mixture_gain,
        mixture_shift,
        router,
        expert_up,
        expert_down,
    )
    micro_count = patches_in.shape[0]
    section_index = lax.axis_index("section")
    section_count = lax.axis_size("section")
    last_section = section_count - 1
    task_rows = jnp.repeat(task_ids, PATCHES, axis=1)
    longest_matrix = max(
        (sum((shards[member].size for member in group)) for group in MATRIX_GROUPS)
    )
    rows_out = []
    for group in MATRIX_GROUPS:
        joined = jnp.concatenate([shards[member].reshape(-1) for member in group], axis=0)
        rows_out.append(jnp.pad(joined, (0, longest_matrix - joined.shape[0])))
    landed_weights = lax.all_to_all(
        jnp.stack(rows_out, axis=0), "section", split_axis=0, concat_axis=0, tiled=True
    )
    matrices = [None] * len(MATRIX_INDEX)
    for group in MATRIX_GROUPS:
        offset = 0
        for member in group:
            count = shards[member].size
            shard_shape = shards[member].shape
            piece = landed_weights[:, offset : offset + count].reshape(
                (section_count,) + shard_shape
            )
            matrices[MATRIX_INDEX.index(member)] = piece.reshape(
                (section_count * shard_shape[0],) + shard_shape[1:]
            )
            offset = offset + count
    params = with_matrices(shards, tuple(matrices))

    def run_first(incoming, micro_index):
        return attend_forward(incoming, *params[0:5])

    def run_dense(incoming, micro_index):
        return dense_forward(incoming, *params[5:11])

    def run_second(incoming, micro_index):
        return attend_forward(incoming, *params[11:16])

    def run_mixture(incoming, micro_index):
        return mixture_forward(
            incoming,
            task_rows[micro_index],
            routes[micro_index],
            keep_mask[micro_index],
            *params[16:21]
        )

    def run_none(incoming, micro_index):
        return jnp.zeros_like(incoming)

    forward_branches = [run_first, run_dense, run_second, run_mixture, run_none]

    def forward_step(step_index, carried):
        arriving, stored, finished = carried
        micro_index = step_index - section_index
        working = (micro_index >= 0) & (micro_index < micro_count)
        clipped = jnp.clip(micro_index, 0, micro_count - 1)
        entering = jnp.where(section_index == 0, patches_in[clipped], arriving)
        stored = stored.at[clipped].set(jnp.where(working, entering, stored[clipped]))
        leaving = lax.switch(
            jnp.where(working, section_index, 4), forward_branches, entering, clipped
        )
        keep_final = working & (section_index == last_section)
        finished = finished.at[clipped].set(jnp.where(keep_final, leaving, finished[clipped]))
        arriving = jax.tree.map(
            lambda part, own: part.astype(own.dtype),
            passed_along(as_sent(leaving), "section", 1),
            leaving,
        )
        return (arriving, stored, finished)

    empty_rows = jnp.zeros_like(patches_in[0])
    empty_all = jnp.zeros_like(patches_in)
    _, stored, finished = lax.fori_loop(
        0, micro_count + last_section, forward_step, (empty_rows, empty_all, empty_all)
    )

    def back_first(incoming, upstream, totals, micro_index):
        passed, gradients = attend_backward(incoming, upstream, *params[0:5])
        return (passed, add_into(totals, 0, gradients))

    def back_dense(incoming, upstream, totals, micro_index):
        passed, gradients = dense_backward(incoming, upstream, *params[5:11])
        return (passed, add_into(totals, 5, gradients))

    def back_second(incoming, upstream, totals, micro_index):
        passed, gradients = attend_backward(incoming, upstream, *params[11:16])
        return (passed, add_into(totals, 11, gradients))

    def back_mixture(incoming, upstream, totals, micro_index):
        passed, gradients = mixture_backward(
            incoming,
            upstream,
            task_rows[micro_index],
            routes[micro_index],
            keep_mask[micro_index],
            *params[16:21]
        )
        return (passed, add_into(totals, 16, gradients))

    def back_none(incoming, upstream, totals, micro_index):
        return (jnp.zeros_like(incoming), totals)

    backward_branches = [back_first, back_dense, back_second, back_mixture, back_none]

    def backward_step(step_index, carried):
        arriving, totals, returned = carried
        micro_index = step_index - (last_section - section_index)
        working = (micro_index >= 0) & (micro_index < micro_count)
        clipped = jnp.clip(micro_index, 0, micro_count - 1)
        upstream = jnp.where(section_index == last_section, cotangent[clipped], arriving)
        passed, totals = lax.switch(
            jnp.where(working, section_index, 4),
            backward_branches,
            stored[clipped],
            upstream,
            totals,
            clipped,
        )
        keep_first = working & (section_index == 0)
        returned = returned.at[clipped].set(jnp.where(keep_first, passed, returned[clipped]))
        arriving = jax.tree.map(
            lambda part, own: part.astype(own.dtype),
            passed_along(as_sent(passed), "section", -1),
            passed,
        )
        return (arriving, totals, returned)

    zero_totals = tuple((jnp.zeros(member.shape, jnp.float32) for member in params))
    _, totals, returned = lax.fori_loop(
        0, micro_count + last_section, backward_step, (empty_rows, zero_totals, empty_all)
    )
    outputs, inputs_part = (
        lax.psum_scatter(
            finished.astype(jnp.float32).astype(jnp.bfloat16),
            "section",
            scatter_dimension=0,
            tiled=True,
        ).astype(jnp.float32),
        lax.psum_scatter(
            returned.astype(jnp.float32).astype(jnp.bfloat16),
            "section",
            scatter_dimension=0,
            tiled=True,
        ).astype(jnp.float32),
    )
    longest = max(
        (
            sum((totals[member].size // section_count for member in range(start, stop)))
            for start, stop in SECTION_GROUPS
        )
    )
    packed = sum(
        (pack_group(totals, start, stop, section_count, longest) for start, stop in SECTION_GROUPS)
    )
    summed = lax.psum(packed, "wide")
    landed = lax.all_to_all(
        summed.astype(jnp.bfloat16), "section", split_axis=0, concat_axis=0, tiled=True
    ).astype(summed.dtype)
    finals = []
    for group_number, bounds in enumerate(SECTION_GROUPS):
        offset = 0
        for member in range(bounds[0], bounds[1]):
            piece_size = totals[member].size // section_count
            piece_shape = (totals[member].shape[0] // section_count,) + totals[member].shape[1:]
            finals.append(landed[group_number, offset : offset + piece_size].reshape(piece_shape))
            offset = offset + piece_size
    return (outputs.astype(jnp.bfloat16), inputs_part.astype(jnp.bfloat16)) + tuple(finals)


def solution(mesh):
    in_specs = (
        P(None, "wide", None),
        P(None, "wide", None),
        P(None, "wide"),
        P(None, "wide", None),
        P(None, "wide", None),
        P(),
        P(),
        P("section", None),
        P("section", None),
        P(),
        P(),
        P(),
        P("section", None),
        P(),
        P("section", None),
        P(),
        P(),
        P(),
        P("section", None),
        P("section", None),
        P(),
        P(),
        P(),
        P("section", None),
        P("section", None, None),
        P("section", None, None),
    )
    out_specs = (
        P("section", "wide", None),
        P("section", "wide", None),
        P("section"),
        P("section"),
        P("section", None),
        P("section", None),
        P("section"),
        P("section"),
        P("section"),
        P("section", None),
        P("section"),
        P("section", None),
        P("section"),
        P("section"),
        P("section"),
        P("section", None),
        P("section", None),
        P("section"),
        P("section"),
        P("section"),
        P("section", None),
        P("section", None, None),
        P("section", None, None),
    )
    return jax.shard_map(local, mesh=mesh, in_specs=in_specs, out_specs=out_specs, check_vma=False)
```

profile of v0, /device:TPU:0, one launch (start us, length us, event | category | flops | bytes accessed | tf_op | source)
XLA Modules:
  0.0 3392.7 jit_solution(1415499269242061156)
XLA Ops:
  12.5 9.5 pad_maximum_fusion.2
  22.0 27.7 stack.50
  52.4 27.9 stack.49
  84.6 27.7 stack.48
  115.0 27.4 stack.47
  142.4 24.3 maximum_bitcast_fusion
  167.3 47.8 %reduce.95 = bf16[4,1180416]{1,0:T(4,128)(2,1)} reduce(bf16[4,1,1180416]{2,0,1:T(4,128)(2,1)} %maximum_bitcast_fusion, bf16[]{:T(256)} %broadcast.1791), dimensions={1}, to_apply=%copy.396.reduce_sub_computation | reduce | bytes 18886658 | tf_op jit(solution)/shard_map/all_to_all | solution.py:370
  215.1 26.7 reshape.975
  241.8 5.9 all-to-all-start
  249.5 103.4 %all-to-all-done = bf16[4,2,590208]{2,1,0:T(2,128)(2,1)} async-done(((bf16[4,2,590208]{2,1,0:T(2,128)(2,1)}), bf16[4,2,590208]{2,1,0:T(2,128)(2,1)}, u32[]{:S(2)}, u32[]{:S(2)}) %all-to-all-start) | async-done | bytes 9443360 | tf_op jit(solution)/shard_map/all_to_all | solution.py:370
  352.9 37.0 %reshape.976 = bf16[4,1,1180416]{2,1,0:T(2,128)(2,1)} reshape(bf16[4,2,590208]{2,1,0:T(2,128)(2,1)} %all-to-all-done) | data formatting | bytes 18886656
  389.9 14.1 copy.467
  405.3 5.8 fusion.345
  429.4 604.0 %while.83 = (s32[]{:T(128)}, bf16[784,384]{1,0:T(8,128)(2,1)S(1)}, bf16[4,784,384]{2,1,0:T(8,128)(2,1)}, bf16[4,784,384]{2,1,0:T(8,128)(2,1)}, s32[]{:T(128)}, /...) while((s32[]{:T(128)}, bf16[784,384]{1,0:T(8,128)(2,1)S(1)}, ...), condition=%wide.region_26.27_spmd.clone, body=%wide.region_0.26_spmd.clone.sunk | while | flops 4867547136 | bytes 68526392 | solution.py:432
  435.0 45.4 %conditional.6 = (bf16[784,384]{1,0:T(8,128)(2,1)}) conditional(s32[]{:T(128)} %clamp.35, (bf16[784,384]{1,0:T(8,128)(2,1)S(1)}, f32[384]{0:T(512)}, f32[384]{0:T(512)}, bf16[384,1152]{1,0:T(8,128)(2,1)}, bf16[384,384]{1,0:T(8,128)(2,1)}, /*index=5*/f32[384]{0:T(512)}) %tuple.225, (bf16[784,384]{1,0:T(8,128)(2,1)S(1)}, ...), branch_computations={%region_1.5_spmd, %region_6.8_spmd, %region_9.13_spmd, %region_14.... | conditional | flops 4866041856 | bytes 58889340 | solution.py:418
  484.6 10.0 collective-permute-done
  500.2 38.0 %conditional.6 = (bf16[784,384]{1,0:T(8,128)(2,1)}) conditional(s32[]{:T(128)} %clamp.35, (bf16[784,384]{1,0:T(8,128)(2,1)S(1)}, f32[384]{0:T(512)}, f32[384]{0:T(512)}, bf16[384,1152]{1,0:T(8,128)(2,1)}, bf16[384,384]{1,0:T(8,128)(2,1)}, /*index=5*/f32[384]{0:T(512)}) %tuple.225, (bf16[784,384]{1,0:T(8,128)(2,1)S(1)}, ...), branch_computations={%region_1.5_spmd, %region_6.8_spmd, %region_9.13_spmd, %region_14.... | conditional | flops 4866041856 | bytes 58889340 | solution.py:418
  542.3 9.4 collective-permute-done
  557.6 45.4 %conditional.6 = (bf16[784,384]{1,0:T(8,128)(2,1)}) conditional(s32[]{:T(128)} %clamp.35, (bf16[784,384]{1,0:T(8,128)(2,1)S(1)}, f32[384]{0:T(512)}, f32[384]{0:T(512)}, bf16[384,1152]{1,0:T(8,128)(2,1)}, bf16[384,384]{1,0:T(8,128)(2,1)}, /*index=5*/f32[384]{0:T(512)}) %tuple.225, (bf16[784,384]{1,0:T(8,128)(2,1)S(1)}, ...), branch_computations={%region_1.5_spmd, %region_6.8_spmd, %region_9.13_spmd, %region_14.... | conditional | flops 4866041856 | bytes 58889340 | solution.py:418
  607.1 8.8 collective-permute-done
  621.5 45.4 %conditional.6 = (bf16[784,384]{1,0:T(8,128)(2,1)}) conditional(s32[]{:T(128)} %clamp.35, (bf16[784,384]{1,0:T(8,128)(2,1)S(1)}, f32[384]{0:T(512)}, f32[384]{0:T(512)}, bf16[384,1152]{1,0:T(8,128)(2,1)}, bf16[384,384]{1,0:T(8,128)(2,1)}, /*index=5*/f32[384]{0:T(512)}) %tuple.225, (bf16[784,384]{1,0:T(8,128)(2,1)S(1)}, ...), branch_computations={%region_1.5_spmd, %region_6.8_spmd, %region_9.13_spmd, %region_14.... | conditional | flops 4866041856 | bytes 58889340 | solution.py:418
  671.0 8.1 collective-permute-done
  684.8 12.6 conditional.6
  697.4 19.1 collective-permute-start
  719.3 7.2 collective-permute-done
  732.5 20.1 conditional.6
  752.5 99.2 %collective-permute-start = (bf16[784,384]{1,0:T(8,128)(2,1)}, bf16[784,384]{1,0:T(8,128)(2,1)S(1)}, u32[]{:S(2)}, u32[]{:S(2)}) collective-permute-start(bf16[784,384]{1,0:T(8,128)(2,1)} %get-tuple-element.4310), channel_id=1, source_target_pairs={{0,8},{8,16},{16,24},{1,9},{9,17},{17,25},{2,10},{10,18},{18,26},{... | collective-permute-start | bytes 1806344 | tf_op jit(solution)/shard_map/while/body/eval_jaxpr/ppermute | solution.py:33
  854.5 6.0 collective-permute-done
  866.1 19.9 conditional.6
  886.0 136.9 %collective-permute-start = (bf16[784,384]{1,0:T(8,128)(2,1)}, bf16[784,384]{1,0:T(8,128)(2,1)S(1)}, u32[]{:S(2)}, u32[]{:S(2)}) collective-permute-start(bf16[784,384]{1,0:T(8,128)(2,1)} %get-tuple-element.4310), channel_id=1, source_target_pairs={{0,8},{8,16},{16,24},{1,9},{9,17},{17,25},{2,10},{10,18},{18,26},{... | collective-permute-start | bytes 1806344 | tf_op jit(solution)/shard_map/while/body/eval_jaxpr/ppermute | solution.py:33
  1055.4 1399.5 %while.84 = (s32[]{:T(128)}, bf16[784,384]{1,0:T(8,128)(2,1)S(1)}, f32[384]{0:T(512)S(1)}, f32[384]{0:T(512)S(1)}, f32[384,1152]{1,0:T(8,128)}, /*index=5*/f32[3...) while((s32[]{:T(128)}, bf16[784,384]{1,0:T(8,128)(2,1)S(1)}, ...), condition=%wide.region_79.80_spmd.clone, body=%wide.region_28.79_spmd.clone.sunk | while | flops 14147868672 | bytes 293206048 | solution.py:488
  1058.3 28.3 conditional.7
  1092.0 108.5 %collective-permute-done.1 = bf16[784,384]{1,0:T(8,128)(2,1)S(1)} collective-permute-done((bf16[784,384]{1,0:T(8,128)(2,1)S(1)}, bf16[784,384]{1,0:T(8,128)(2,1)S(1)}, u32[]{:S(2)}, u32[]{:S(2)}) %collective-permute-start.1) | collective-permute-done | bytes 602144 | tf_op jit(solution)/shard_map/while/body/eval_jaxpr/ppermute | solution.py:33
  1203.1 27.8 conditional.7
  1236.4 127.7 %collective-permute-done.1 = bf16[784,384]{1,0:T(8,128)(2,1)S(1)} collective-permute-done((bf16[784,384]{1,0:T(8,128)(2,1)S(1)}, bf16[784,384]{1,0:T(8,128)(2,1)S(1)}, u32[]{:S(2)}, u32[]{:S(2)}) %collective-permute-start.1) | collective-permute-done | bytes 602144 | tf_op jit(solution)/shard_map/while/body/eval_jaxpr/ppermute | solution.py:33
  1366.7 28.1 conditional.7
  1400.4 271.8 %collective-permute-done.1 = bf16[784,384]{1,0:T(8,128)(2,1)S(1)} collective-permute-done((bf16[784,384]{1,0:T(8,128)(2,1)S(1)}, bf16[784,384]{1,0:T(8,128)(2,1)S(1)}, u32[]{:S(2)}, u32[]{:S(2)}) %collective-permute-start.1) | collective-permute-done | bytes 602144 | tf_op jit(solution)/shard_map/while/body/eval_jaxpr/ppermute | solution.py:33
  1674.9 79.3 %conditional.7 = (bf16[784,384]{1,0:T(8,128)(2,1)S(1)}, f32[384]{0:T(512)S(1)}, f32[384]{0:T(512)S(1)}, f32[384,1152]{1,0:T(8,128)}, f32[384,384]{1,0:T(8,128)},...) conditional(s32[]{:T(128)} %clamp.36, ...), branch_computations={%region_29.39_spmd, %region_40.0_spmd, %region_49.59_spmd, %region... | conditional | flops 14146965504 | bytes 284773760 | solution.py:470
  1759.7 140.5 %collective-permute-done.1 = bf16[784,384]{1,0:T(8,128)(2,1)S(1)} collective-permute-done((bf16[784,384]{1,0:T(8,128)(2,1)S(1)}, bf16[784,384]{1,0:T(8,128)(2,1)S(1)}, u32[]{:S(2)}, u32[]{:S(2)}) %collective-permute-start.1) | collective-permute-done | bytes 602144 | tf_op jit(solution)/shard_map/while/body/eval_jaxpr/ppermute | solution.py:33
  1902.8 79.3 %conditional.7 = (bf16[784,384]{1,0:T(8,128)(2,1)S(1)}, f32[384]{0:T(512)S(1)}, f32[384]{0:T(512)S(1)}, f32[384,1152]{1,0:T(8,128)}, f32[384,384]{1,0:T(8,128)},...) conditional(s32[]{:T(128)} %clamp.36, ...), branch_computations={%region_29.39_spmd, %region_40.0_spmd, %region_49.59_spmd, %region... | conditional | flops 14146965504 | bytes 284773760 | solution.py:470
  1987.6 138.2 %collective-permute-done.1 = bf16[784,384]{1,0:T(8,128)(2,1)S(1)} collective-permute-done((bf16[784,384]{1,0:T(8,128)(2,1)S(1)}, bf16[784,384]{1,0:T(8,128)(2,1)S(1)}, u32[]{:S(2)}, u32[]{:S(2)}) %collective-permute-start.1) | collective-permute-done | bytes 602144 | tf_op jit(solution)/shard_map/while/body/eval_jaxpr/ppermute | solution.py:33
  2128.3 78.9 %conditional.7 = (bf16[784,384]{1,0:T(8,128)(2,1)S(1)}, f32[384]{0:T(512)S(1)}, f32[384]{0:T(512)S(1)}, f32[384,1152]{1,0:T(8,128)}, f32[384,384]{1,0:T(8,128)},...) conditional(s32[]{:T(128)} %clamp.36, ...), branch_computations={%region_29.39_spmd, %region_40.0_spmd, %region_49.59_spmd, %region... | conditional | flops 14146965504 | bytes 284773760 | solution.py:470
  2212.7 141.1 %collective-permute-done.1 = bf16[784,384]{1,0:T(8,128)(2,1)S(1)} collective-permute-done((bf16[784,384]{1,0:T(8,128)(2,1)S(1)}, bf16[784,384]{1,0:T(8,128)(2,1)S(1)}, u32[]{:S(2)}, u32[]{:S(2)}) %collective-permute-start.1) | collective-permute-done | bytes 602144 | tf_op jit(solution)/shard_map/while/body/eval_jaxpr/ppermute | solution.py:33
  2356.5 79.2 %conditional.7 = (bf16[784,384]{1,0:T(8,128)(2,1)S(1)}, f32[384]{0:T(512)S(1)}, f32[384]{0:T(512)S(1)}, f32[384,1152]{1,0:T(8,128)}, f32[384,384]{1,0:T(8,128)},...) conditional(s32[]{:T(128)} %clamp.36, ...), branch_computations={%region_29.39_spmd, %region_40.0_spmd, %region_49.59_spmd, %region... | conditional | flops 14146965504 | bytes 284773760 | solution.py:470
  2441.2 6.4 collective-permute-done.1
  2459.2 13.4 copy.456
  2472.6 18.0 copy.457
  2523.1 10.5 dynamic-update-slice.34
  2536.4 13.2 dynamic-update-slice.39
  2559.5 10.5 dynamic-update-slice.45
  2575.6 49.6 %dynamic-update-slice.30 = f32[4,1180608]{1,0:T(4,128)} dynamic-update-slice(f32[4,1180608]{1,0:T(4,128)} %dynamic-update-slice.29, f32[4,589824]{1,0:T(4,128)} %bitcast.322, s32[]{} %constant.748, s32[]{} %constant.751) | dynamic-update-slice | bytes 18874372
  2625.2 49.4 %dynamic-update-slice.31 = f32[4,1180608]{1,0:T(4,128)} dynamic-update-slice(f32[4,1180608]{1,0:T(4,128)} %dynamic-update-slice.30, f32[4,589824]{1,0:T(4,128)} %bitcast.321, s32[]{} %constant.748, s32[]{} %constant.752) | dynamic-update-slice | bytes 18874372 | tf_op jit(solution)/shard_map/concatenate | solution.py:296
  2674.6 12.8 dynamic-update-slice.41
  2688.8 29.1 add_add_fusion.4
  2718.0 370.6 %all-reduce.16 = bf16[4,1180608]{1,0:T(4,128)(2,1)} all-reduce(f32[4,1180608]{1,0:T(4,128)} %add_add_fusion.4), channel_id=1, replica_groups=mesh['section'=4,'wide'=8] {'wide'}, use_global_device_ids=true, to_apply=%region_81.82 | all-reduce | flops 4722432 | bytes 28334592 | tf_op jit(solution)/shard_map/psum | solution.py:514
  3088.6 45.3 %reduce.96 = bf16[4,1180608]{1,0:T(4,128)(2,1)} reduce(bf16[4,1,1180608]{2,0,1:T(4,128)(2,1)} %bitcast.320, bf16[]{:T(256)} %broadcast.1791), dimensions={1}, to_apply=%copy.402.reduce_sub_computation | reduce | bytes 18889730 | tf_op jit(solution)/shard_map/all_to_all | solution.py:515
  3134.0 22.6 reshape.977
  3156.6 5.8 all-to-all-start.1
  3163.9 121.5 %all-to-all-done.1 = bf16[4,2,590304]{2,1,0:T(2,128)(2,1)} async-done(((bf16[4,2,590304]{2,1,0:T(2,128)(2,1)}), bf16[4,2,590304]{2,1,0:T(2,128)(2,1)}, u32[]{:S(2)}, u32[]{:S(2)}) %all-to-all-start.1) | async-done | bytes 9444896 | tf_op jit(solution)/shard_map/all_to_all | solution.py:515
  3285.4 24.3 reshape.978
  3309.6 14.0 copy.466
  3323.7 6.5 copy-done.12
  3336.1 7.9 slice_reduce_fusion.4
  3349.0 28.7 slice_reduce_fusion.2
  (588 shorter events, 620.1 us)
Async XLA Ops:
  7.2 5.1 copy-start.79
  22.0 27.8 copy-start.69
  22.0 27.8 copy-start.46
  50.1 30.3 copy-start.44
  50.1 30.4 copy-start.45
  80.9 31.4 copy-start.70
  80.9 31.5 copy-start.47
  84.6 57.8 %slice-start.6 = ((s8[4721664]{0:T(1024)(128)(4,1)}), s8[527360]{0:T(1024)(128)(4,1)S(1)}, s32[]{:S(2)}) async-start(s8[4721664]{0:T(1024)(128)(4,1)} %bitcast.331), calls=%async_computation.12 | async-start | bytes 1054720
  112.6 29.8 slice-start.7
  112.6 29.8 copy-start.25
  241.8 6.0 copy-start.72
  241.8 111.1 %all-to-all-start = ((bf16[4,2,590208]{2,1,0:T(2,128)(2,1)}), bf16[4,2,590208]{2,1,0:T(2,128)(2,1)}, u32[]{:S(2)}, u32[]{:S(2)}) async-start(bf16[4,2,590208]{2,1,0:T(2,128)(2,1)} %reshape.975), calls=%async_computation | async-start | bytes 18886656 | tf_op jit(solution)/shard_map/all_to_all | solution.py:370
  417.4 5.9 slice-start.8
  417.7 5.7 slice-start.9
  480.4 14.2 collective-permute-start
  538.2 13.5 collective-permute-start
  603.0 12.9 collective-permute-start
  666.9 12.2 collective-permute-start
  697.4 29.1 collective-permute-start
  752.5 108.0 %collective-permute-start = (bf16[784,384]{1,0:T(8,128)(2,1)}, bf16[784,384]{1,0:T(8,128)(2,1)S(1)}, u32[]{:S(2)}, u32[]{:S(2)}) collective-permute-start(bf16[784,384]{1,0:T(8,128)(2,1)} %get-tuple-element.4310), channel_id=1, source_target_pairs={{0,8},{8,16},{16,24},{1,9},{9,17},{17,25},{2,10},{10,18},{18,26},{... | collective-permute-start | bytes 1806344 | tf_op jit(solution)/shard_map/while/body/eval_jaxpr/ppermute | solution.py:33
  886.0 144.8 %collective-permute-start = (bf16[784,384]{1,0:T(8,128)(2,1)}, bf16[784,384]{1,0:T(8,128)(2,1)S(1)}, u32[]{:S(2)}, u32[]{:S(2)}) collective-permute-start(bf16[784,384]{1,0:T(8,128)(2,1)} %get-tuple-element.4310), channel_id=1, source_target_pairs={{0,8},{8,16},{16,24},{1,9},{9,17},{17,25},{2,10},{10,18},{18,26},{... | collective-permute-start | bytes 1806344 | tf_op jit(solution)/shard_map/while/body/eval_jaxpr/ppermute | solution.py:33
  1033.5 8.0 copy-start.35
  1086.6 114.0 %collective-permute-start.1 = (bf16[784,384]{1,0:T(8,128)(2,1)S(1)}, bf16[784,384]{1,0:T(8,128)(2,1)S(1)}, u32[]{:S(2)}, u32[]{:S(2)}) collective-permute-start(bf16[784,384]{1,0:T(8,128)(2,1)S(1)} %get-tuple-element.3905), channel_id=1, source_target_pairs={{8,0},{16,8},{24,16},{9,1},{17,9},{25,17},{10,2},{18,10},{26,18},{... | collective-permute-start | bytes 1806344 | tf_op jit(solution)/shard_map/while/body/eval_jaxpr/ppermute | solution.py:33
  1230.9 133.2 %collective-permute-start.1 = (bf16[784,384]{1,0:T(8,128)(2,1)S(1)}, bf16[784,384]{1,0:T(8,128)(2,1)S(1)}, u32[]{:S(2)}, u32[]{:S(2)}) collective-permute-start(bf16[784,384]{1,0:T(8,128)(2,1)S(1)} %get-tuple-element.3905), channel_id=1, source_target_pairs={{8,0},{16,8},{24,16},{9,1},{17,9},{25,17},{10,2},{18,10},{26,18},{... | collective-permute-start | bytes 1806344 | tf_op jit(solution)/shard_map/while/body/eval_jaxpr/ppermute | solution.py:33
  1394.9 277.3 %collective-permute-start.1 = (bf16[784,384]{1,0:T(8,128)(2,1)S(1)}, bf16[784,384]{1,0:T(8,128)(2,1)S(1)}, u32[]{:S(2)}, u32[]{:S(2)}) collective-permute-start(bf16[784,384]{1,0:T(8,128)(2,1)S(1)} %get-tuple-element.3905), channel_id=1, source_target_pairs={{8,0},{16,8},{24,16},{9,1},{17,9},{25,17},{10,2},{18,10},{26,18},{... | collective-permute-start | bytes 1806344 | tf_op jit(solution)/shard_map/while/body/eval_jaxpr/ppermute | solution.py:33
  1721.2 5.0 copy-start.10
  1721.3 11.1 slice-start.2
  1724.8 7.6 slice-start.3
  1726.3 6.1 copy-start.21
  1754.2 146.0 %collective-permute-start.1 = (bf16[784,384]{1,0:T(8,128)(2,1)S(1)}, bf16[784,384]{1,0:T(8,128)(2,1)S(1)}, u32[]{:S(2)}, u32[]{:S(2)}) collective-permute-start(bf16[784,384]{1,0:T(8,128)(2,1)S(1)} %get-tuple-element.3905), channel_id=1, source_target_pairs={{8,0},{16,8},{24,16},{9,1},{17,9},{25,17},{10,2},{18,10},{26,18},{... | collective-permute-start | bytes 1806344 | tf_op jit(solution)/shard_map/while/body/eval_jaxpr/ppermute | solution.py:33
  1949.1 11.1 slice-start.2
  1952.6 7.6 slice-start.3
  1954.1 6.1 copy-start.21
  1982.1 143.7 %collective-permute-start.1 = (bf16[784,384]{1,0:T(8,128)(2,1)S(1)}, bf16[784,384]{1,0:T(8,128)(2,1)S(1)}, u32[]{:S(2)}, u32[]{:S(2)}) collective-permute-start(bf16[784,384]{1,0:T(8,128)(2,1)S(1)} %get-tuple-element.3905), channel_id=1, source_target_pairs={{8,0},{16,8},{24,16},{9,1},{17,9},{25,17},{10,2},{18,10},{26,18},{... | collective-permute-start | bytes 1806344 | tf_op jit(solution)/shard_map/while/body/eval_jaxpr/ppermute | solution.py:33
  2174.2 11.1 slice-start.2
  2177.7 7.6 slice-start.3
  2179.3 6.1 copy-start.21
  2207.2 146.6 %collective-permute-start.1 = (bf16[784,384]{1,0:T(8,128)(2,1)S(1)}, bf16[784,384]{1,0:T(8,128)(2,1)S(1)}, u32[]{:S(2)}, u32[]{:S(2)}) collective-permute-start(bf16[784,384]{1,0:T(8,128)(2,1)S(1)} %get-tuple-element.3905), channel_id=1, source_target_pairs={{8,0},{16,8},{24,16},{9,1},{17,9},{25,17},{10,2},{18,10},{26,18},{... | collective-permute-start | bytes 1806344 | tf_op jit(solution)/shard_map/while/body/eval_jaxpr/ppermute | solution.py:33
  2402.8 11.1 slice-start.2
  2406.3 7.6 slice-start.3
  2407.8 6.1 copy-start.21
  2435.7 11.9 collective-permute-start.1
  2454.9 17.7 copy-start.52
  2454.9 17.7 copy-start.54
  2454.9 17.7 copy-start.55
  2454.9 17.7 copy-start.56
  2472.6 18.0 copy-start.59
  2472.6 18.7 copy-start.62
  2472.6 23.1 copy-start.18
  2492.0 13.3 copy-start.9
  2504.7 9.5 copy-start.15
  2505.3 10.0 copy-start.53
  2507.8 28.6 copy-start.29
  2510.6 10.9 copy-start.71
  2523.1 30.8 copy-start.77
  2523.1 32.2 copy-start.73
  2536.4 33.5 copy-start.34
  2536.4 37.8 %copy-start.78 = (f32[4,96]{1,0:T(4,128)S(1)}, f32[4,96]{1,0:T(4,128)}, u32[]{:S(2)}) copy-start(f32[4,96]{1,0:T(4,128)} %reshape.786) | copy-start | bytes 4612
  2625.2 49.4 %copy-start.26 = (f32[4,147456]{1,0:T(4,128)S(1)}, f32[4,147456]{1,0:T(4,128)}, u32[]{:S(2)}) copy-start(f32[4,147456]{1,0:T(4,128)} %reshape.791) | copy-start | bytes 7077892
  2674.6 12.8 copy-start.76
  3156.6 128.8 %all-to-all-start.1 = ((bf16[4,2,590304]{2,1,0:T(2,128)(2,1)}), bf16[4,2,590304]{2,1,0:T(2,128)(2,1)}, u32[]{:S(2)}, u32[]{:S(2)}) async-start(bf16[4,2,590304]{2,1,0:T(2,128)(2,1)} %reshape.977), calls=%async_computation.1 | async-start | bytes 18890752 | tf_op jit(solution)/shard_map/all_to_all | solution.py:515
  3162.4 223.3 %reduce-scatter.7.cloned.1.call-start = ((), (), s32[]{:S(2)}) async-start(), calls=%async_computation.4 | async-start | bytes 3010560
  3163.1 222.5 %reduce-scatter.9.cloned.1.call-start = ((), (), s32[]{:S(2)}) async-start(), calls=%async_computation.5 | async-start | bytes 3010560
  3323.7 6.5 copy-start.12
  (41 other events, 112.4 us)
Sparse Core Ops, SparseCore 0:
  3166.8 95.9 reduce-scatter.6
  3266.7 60.2 reduce-scatter.8
where the time goes:
time: 3410 us; the launch traced here: 3390 us
  waiting for transfers between devices  1220 us (36%)
  local copies, waits for them, and re-layouts  819 us (24%)
  blocking collectives  371 us (11%)
  other arithmetic  289 us (8%)
  starting transfers between devices  281 us (8%)
  loops' own time  280 us (8%)
  matrix products  123 us (4%)
    ppermute x14, waiting for transfers between devices, passed_along(): return lax.ppermute(block, axis, route)  989 us
    psum x1, blocking collectives, local(): summed = lax.psum(packed, 'wide')  371 us
    unnamed x109, local copies, waits for them, and re-layouts  307 us
    ppermute x14, starting transfers between devices, passed_along(): return lax.ppermute(block, axis, route)  270 us
    another operation x7, loops' own time, backward_step(): lax.switch(jnp.where(working, section_index, 4), backward_branches, store...  160 us
    all_to_all x1, waiting for transfers between devices, local(): lax.all_to_all(summed.astype(jnp.bfloat16), 'section', split_axis=0, conc...  121 us
    another operation x4, local copies, waits for them, and re-layouts, local(): jnp.stack(rows_out, axis=0)  111 us
    another operation x7, loops' own time, forward_step(): lax.switch(jnp.where(working, section_index, 4), forward_branches, enteri...  105 us
  transfers between devices with their start and end apart: 18, of which 16 were waited for; matrix products, arithmetic and copies ran while one was open for 4% of the time, Pallas kernels for 0%

commit v1 on v0

v1 whole, which is shorter than its diff:
```python
import functools

import jax
import jax.numpy as jnp
from jax import lax
from jax.experimental import pallas as pl
from jax.experimental.pallas import tpu as pltpu
from jax.sharding import PartitionSpec as P

HEADS = 6
HEAD_DIM = 64
PATCHES = 196
EXPERTS = 4
TASKS = 2
CAPACITY = 488
EPSILON = 1e-06
MESH = pl.DeviceIdType.MESH
bf16 = jnp.bfloat16
f32 = jnp.float32

RP = 208
SL = 496
VROWS = 32
NSEM = 120


def dot(left, right):
    return jnp.dot(left, right, preferred_element_type=f32)


def nt(left, right):
    return lax.dot_general(left, right, (((1,), (1,)), ((), ())), preferred_element_type=f32)


def tn(left, right):
    return lax.dot_general(left, right, (((0,), (0,)), ((), ())), preferred_element_type=f32)


def iota(shape, dim):
    return lax.broadcasted_iota(jnp.int32, shape, dim)


def onehot(cond):
    return jnp.where(cond, 1.0, 0.0).astype(bf16)


def normed(x):
    centered = x - jnp.mean(x, axis=-1, keepdims=True)
    scale = lax.rsqrt(jnp.mean(centered * centered, axis=-1, keepdims=True) + EPSILON)
    return centered * scale, scale


def norm_back(grad, xhat, scale, gain):
    inner = grad * gain
    mean_inner = jnp.mean(inner, axis=-1, keepdims=True)
    mean_cross = jnp.mean(inner * xhat, axis=-1, keepdims=True)
    return scale * (inner - mean_inner - xhat * mean_cross)


def gelu_both(u):
    cdf = 0.5 * (1.0 + lax.erf(u * 0.7071067811865476))
    return u * cdf, cdf + u * (jnp.exp(u * u * -0.5) * 0.3989422804014327)


def column_sum(v):
    return jnp.sum(v, axis=0, keepdims=True)


V_A1, V_D, V_HB, V_A2, V_M, V_R = 0, 3, 6, 10, 13, 16


class Links:
    def __init__(self, send_sems, recv_sems):
        self.send_sems, self.recv_sems, self.used, self.sent = send_sems, recv_sems, 0, []

    def take(self, count=1):
        first = self.used
        self.used += count
        return first

    def copy(self, number, src, dst, device):
        return pltpu.make_async_remote_copy(
            src_ref=src,
            dst_ref=dst,
            send_sem=self.send_sems.at[number],
            recv_sem=self.recv_sems.at[number],
            device_id=device,
            device_id_type=MESH,
        )

    def start(self, number, src, dst, device):
        made = self.copy(number, src, dst, device)
        made.start()
        self.sent.append(made)
        return made

    def forget(self, made):
        self.sent = [other for other in self.sent if other is not made]


def block_kernel(bits, refs):
    r = refs
    R, D = r.patches.shape[1:]
    FF = r.up.shape[1]
    xraw = r.h3.at[pl.ds(0, R)]
    IMG = R // PATCHES
    RT = IMG * RP
    FC = D
    NF = FF // FC
    sec = lax.axis_index("section")
    wide = lax.axis_index("wide")
    core = lax.rem(wide, 2)
    chip = wide // 2
    NS = 4
    links = Links(r.send, r.recv)

    def section_peer(j):
        hi, lo = sec // 2, lax.rem(sec, 2)
        jh, jl = j // 2, j % 2 if isinstance(j, int) else lax.rem(j, 2)
        return (hi + jh - 2 * hi * jh) * 2 + (lo + jl - 2 * lo * jl)

    def at_section(j):
        return (section_peer(j), wide)

    mate = (sec, wide + 1 - 2 * core)

    def bit_of(b):
        return lax.rem(chip // (1 << b), 2)

    def at_chip(b):
        return (sec, wide + (1 - 2 * bit_of(b)) * (2 << b))

    local = []

    def fetch(src, dst):
        c = pltpu.make_async_copy(src, dst, r.local.at[len(local)])
        c.start()
        local.append(c)
        return c

    fetch_x = fetch(r.patches.at[sec], xraw)
    fetch_c = [fetch(r.cotangent.at[m], r.pool.at[pl.ds(m * R, R)]) for m in range(NS)]
    shards = [
        (r.s_p1, r.w_p1),
        (r.s_o1, r.w_o1),
        (r.s_up, r.w_up),
        (r.s_dn, r.w_dn),
        (r.s_p2, r.w_p2),
        (r.s_o2, r.w_o2),
        (r.s_rt, r.w_rt),
    ]
    fetch_w = []
    for shard, whole in shards:
        n = shard.shape[0]
        fetch_w.append(fetch(shard, whole.at[pl.ds(pl.multiple_of(sec * n, n), n)]))
    fetch_up = fetch(r.expert_up.at[0], r.up)
    fetch_dn = fetch(r.expert_down.at[0], r.down)

    barrier = pltpu.get_barrier_semaphore()
    partners = [at_section(j) for j in range(1, NS)] + [mate] + [at_chip(b) for b in range(bits)]
    for device in partners:
        pl.semaphore_signal(barrier, inc=1, device_id=device, device_id_type=MESH)
    pl.semaphore_wait(barrier, len(partners))

    direct, passed = [], []
    for shard, whole in shards:
        n = shard.shape[0]
        h = n // 2
        numbers = []
        for j in range(1, NS):
            number = links.take()
            links.start(
                number,
                shard.at[pl.ds(pl.multiple_of(core * h, h), h)],
                whole.at[pl.ds(pl.multiple_of(sec * n + core * h, h), h)],
                at_section(j),
            )
            numbers.append(number)
        direct.append(numbers)
        passed.append([links.take() for _ in range(1, NS)])

    def pass_on(group):
        for t in group:
            shard, whole = shards[t]
            n = shard.shape[0]
            h = n // 2
            for j in range(1, NS):
                here = whole.at[pl.ds(pl.multiple_of(section_peer(j) * n + core * h, h), h)]
                links.copy(direct[t][j - 1], here, here, at_section(j)).wait_recv()
                links.start(passed[t][j - 1], here, here, mate)

    def landed(group):
        for t in group:
            shard, whole = shards[t]
            n = shard.shape[0]
            h = n // 2
            fetch_w[t].wait()
            for j in range(1, NS):
                there = whole.at[pl.ds(pl.multiple_of(section_peer(j) * n + (1 - core) * h, h), h)]
                links.copy(passed[t][j - 1], there, there, mate).wait_recv()

    expert_rows = []
    for j in range(NS):
        other = section_peer(j)
        r0 = jnp.zeros((1, R), jnp.int32)
        r1, k0, k1 = r0, r0, r0
        for m in range(NS):
            mine = jnp.where(sec == m, 1, 0)
            r0 = r0 + mine * r.routes[m, 0:1, :]
            r1 = r1 + mine * r.routes[m, 1:2, :]
            k0 = k0 + mine * r.keep[m, 0:1, :]
            k1 = k1 + mine * r.keep[m, 1:2, :]
        expert_rows.append(((r0 == other) & (k0 == 1)) | ((r1 == other) & (k1 == 1)))
    for j in range(NS):
        other = section_peer(j)
        r0 = jnp.zeros((1, R), jnp.int32)
        r1, k0, k1 = r0, r0, r0
        for m in range(NS):
            mine = jnp.where(other == m, 1, 0)
            r0 = r0 + mine * r.routes[m, 0:1, :]
            r1 = r1 + mine * r.routes[m, 1:2, :]
            k0 = k0 + mine * r.keep[m, 0:1, :]
            k1 = k1 + mine * r.keep[m, 1:2, :]
        expert_rows.append(((r0 == sec) & (k0 == 1)) | ((r1 == sec) & (k1 == 1)))
    for k in range(16):
        if k < 8:
            r.chosen[k : k + 1, :] = jnp.where(expert_rows[k], 1.0, 0.0)
        else:
            r.chosen[k : k + 1, :] = jnp.zeros((1, R), f32)

    def slots_of(limit, valid):
        chosen = r.chosen[...].astype(bf16)
        column = iota((limit.shape[0], R), 1)
        before = nt(onehot(column < limit), chosen)
        upto = nt(onehot((column <= limit) & valid), chosen)
        return jnp.where(upto > before, before, -1.0)

    def slots_padded(i, carry):
        off = iota((RP, 1), 0)
        r.pos_pad[pl.ds(pl.multiple_of(i * RP, RP), RP), :] = slots_of(i * PATCHES + off, off < PATCHES)
        return carry

    lax.fori_loop(0, IMG, slots_padded, 0)
    RC = R // 7

    def slots_raw(i, carry):
        off = iota((RC, 1), 0)
        r.pos_raw[pl.ds(pl.multiple_of(i * RC, RC), RC), :] = slots_of(i * RC + off, off >= 0)
        return carry

    lax.fori_loop(0, 7, slots_raw, 0)

    fetch_x.wait()
    for c in fetch_c:
        c.wait()
    for i in range(IMG):
        start = (PATCHES * i) // 16 * 16
        gap = PATCHES * i - start
        a, b = iota((RP, RP), 0), iota((RP, RP), 1)
        shift = onehot((b == a + gap) & (a < PATCHES))
        r.h0[i * RP : (i + 1) * RP, :] = dot(shift, xraw[start : start + RP, :]).astype(bf16)
        first = pl.multiple_of(sec * R + start, 16)
        r.g3[i * RP : (i + 1) * RP, :] = dot(shift, r.pool[pl.ds(first, RP), :]).astype(bf16)

    slot_lane = iota((1, SL), 1).astype(f32)
    for j in range(NS):
        m = section_peer(j)
        pick = onehot(r.pos_raw[:, 4 + j : 5 + j] == slot_lane)
        first = pl.multiple_of(m * R, 16)
        r.gslot[j] = tn(pick, r.pool[pl.ds(first, R), :]).astype(bf16)
        row = iota((R, 128), 0)
        task = jnp.zeros((R, 128), jnp.int32)
        for i in range(IMG):
            task = jnp.where((row >= i * PATCHES) & (row < (i + 1) * PATCHES), r.task[m, i], task)
        r.tslot[j] = tn(pick, task.astype(f32).astype(bf16)).astype(bf16)

    low_half = iota((1, 128), 1) < 64
    half_masks = [onehot(low_half), onehot(jnp.logical_not(low_half))]
    low_half_rows = iota((RP, 128), 1) < 64
    key_ok = iota((RP, RP), 0) < PATCHES

    def attend(h_in, h_out, vecs, w_p, w_o, qkv_s, p_s, ctx_s):
        gain, shift, bias = vecs

        def image(i, carry):
            rows = pl.ds(pl.multiple_of(i * RP, RP), RP)
            x = h_in[rows, :].astype(f32)
            a = (normed(x)[0] * gain[...] + shift[...]).astype(bf16)
            qkv = dot(a, w_p[...]).astype(bf16)
            qkv_s[rows, :] = qkv
            parts = []
            for pair in range(HEADS // 2):
                at = 128 * pair
                q2 = qkv[:, at : at + 128]
                k2 = qkv[:, D + at : D + at + 128]
                v2 = qkv[:, 2 * D + at : 2 * D + at + 128]
                outs = []
                for half in range(2):
                    scores = nt(k2 * half_masks[half], q2)
                    scores = jnp.where(key_ok, scores, -1e30)
                    top = jnp.max(scores, axis=0, keepdims=True)
                    e = jnp.exp((scores - top) * HEAD_DIM**-0.5)
                    p = (e * (1.0 / jnp.sum(e, axis=0, keepdims=True))).astype(bf16)
                    p_s[i * HEADS + 2 * pair + half] = p
                    outs.append(tn(p, v2))
                parts.append(jnp.where(low_half_rows, outs[0], outs[1]).astype(bf16))
            ctx = jnp.concatenate(parts, axis=1)
            ctx_s[rows, :] = ctx
            h_out[rows, :] = (x + dot(ctx, w_o[...]) + bias[...]).astype(bf16)
            return carry

        lax.fori_loop(0, IMG, image, 0)

    def attend_back(h_in, g_in, g_out, vecs, w_p, w_o, qkv_s, p_s, ctx_s, vrow):
        gain, shift, _ = vecs

        def image(i, carry):
            rows = pl.ds(pl.multiple_of(i * RP, RP), RP)
            g = g_in[rows, :]
            gf = g.astype(f32)
            xhat, scale = normed(h_in[rows, :].astype(f32))
            r.a_s[rows, :] = (xhat * gain[...] + shift[...]).astype(bf16)
            gc = nt(g, w_o[...]).astype(bf16)
            qkv = qkv_s[rows, :]
            gq, gk, gv = [], [], []
            for pair in range(HEADS // 2):
                at = 128 * pair
                q2 = qkv[:, at : at + 128]
                k2 = qkv[:, D + at : D + at + 128]
                v2 = qkv[:, 2 * D + at : 2 * D + at + 128]
                gc2 = gc[:, at : at + 128]
                two = []
                for half in range(2):
                    p = p_s[i * HEADS + 2 * pair + half]
                    pf = p.astype(f32)
                    gp = nt(v2 * half_masks[half], gc2)
                    t = pf * gp
                    gs = (t - pf * jnp.sum(t, axis=0, keepdims=True)).astype(bf16)
                    two.append((tn(gs, k2), dot(gs, q2), dot(p, gc2)))
                gq.append((jnp.where(low_half_rows, two[0][0], two[1][0]) * HEAD_DIM**-0.5).astype(bf16))
                gk.append((jnp.where(low_half_rows, two[0][1], two[1][1]) * HEAD_DIM**-0.5).astype(bf16))
                gv.append(jnp.where(low_half_rows, two[0][2], two[1][2]).astype(bf16))
            gqkv = jnp.concatenate(gq + gk + gv, axis=1)
            qkv_s[rows, :] = gqkv
            ga = nt(gqkv, w_p[...])
            r.vec[vrow : vrow + 1, :] += column_sum(ga * xhat)
            r.vec[vrow + 1 : vrow + 2, :] += column_sum(ga)
            r.vec[vrow + 2 : vrow + 3, :] += column_sum(gf)
            g_out[rows, :] = (gf + norm_back(ga, xhat, scale, gain[...])).astype(bf16)
            return carry

        lax.fori_loop(0, IMG, image, 0)

    r.vec[...] = jnp.zeros(r.vec.shape, f32)
    att1 = (r.first_gain, r.first_shift, r.first_bias)
    att2 = (r.second_gain, r.second_shift, r.second_bias)

    pass_on((0, 1))
    landed((0, 1))
    attend(r.h0, r.h1, att1, r.w_p1, r.w_o1, r.qkv1, r.p1, r.ctx1)

    pass_on((2, 3))
    landed((2, 3))
    HR = RT // 2

    def dense_step(i, carry):
        rows = pl.ds(pl.multiple_of(i * HR, HR), HR)
        x = r.h1[rows, :].astype(f32)
        a = (normed(x)[0] * r.dense_gain[...] + r.dense_shift[...]).astype(bf16)
        total = x + r.dense_bias[...]
        for f in range(NF):
            cols = slice(f * FC, (f + 1) * FC)
            u = dot(a, r.w_up[:, cols]) + r.hidden_bias[:, cols]
            z, slope = gelu_both(u)
            z = z.astype(bf16)
            r.z[rows, cols] = z
            r.slope[rows, cols] = slope.astype(bf16)
            total = total + dot(z, r.w_dn[cols, :])
        r.h2[rows, :] = total.astype(bf16)
        return carry

    lax.fori_loop(0, 2, dense_step, 0)

    pass_on((4, 5, 6))
    landed((4, 5, 6))
    attend(r.h2, r.h3, att2, r.w_p2, r.w_o2, r.qkv2, r.p2, r.ctx2)

    lane = iota((1, 128), 1)

    def gates_of(a, task):
        logits = dot(a, r.w_rt[...])
        active = (lane < TASKS * EXPERTS) & (lane // EXPERTS == task)
        top = jnp.max(jnp.where(active, logits, -1e30), axis=-1, keepdims=True)
        e = jnp.where(active, jnp.exp(jnp.minimum(logits - top, 0.0)), 0.0)
        return e / jnp.sum(e, axis=-1, keepdims=True), active

    def mix_rows(i, carry):
        rows = pl.ds(pl.multiple_of(i * RP, RP), RP)
        a = (normed(r.h3[rows, :].astype(f32))[0] * r.mixture_gain[...] + r.mixture_shift[...]).astype(bf16)
        r.a4[rows, :] = a
        task = jnp.zeros((RP, 1), jnp.int32) + r.task[sec, i]
        r.gates[rows, :] = gates_of(a, task)[0]
        return carry

    lax.fori_loop(0, IMG, mix_rows, 0)

    slots_first = links.take(NS)
    for j in (3, 1, 2, 0):
        pick = onehot(r.pos_pad[:, j : j + 1] == slot_lane)
        r.slot_out[j] = tn(pick, r.a4[...]).astype(bf16)
        if j > 0:
            links.start(slots_first + j, r.slot_out.at[j], r.slot_in.at[j], at_section(j))
        else:
            r.slot_in[0] = r.slot_out[0]

    fetch_up.wait()
    fetch_dn.wait()
    r.eg[...] = jnp.zeros(r.eg.shape, f32)
    ga_first, q_first, w_first = links.take(NS), links.take(NS), links.take(NS)

    def ga_in(j):
        return r.pool.at[pl.ds((j - 1) * SL, SL)]

    def w_in(j):
        return r.pool.at[pl.ds((j + 2) * SL, SL)]

    def expert_step(j, carry):
        there = at_section(j)

        @pl.when(j > 0)
        def _():
            links.copy(slots_first + j, r.slot_out.at[j], r.slot_in.at[j], there).wait()

        a = r.slot_in[j]
        gs = r.gslot[j]
        gates, active = gates_of(a, r.tslot[j][:, 0:1].astype(jnp.int32))
        combine = jnp.sum(jnp.where(lax.rem(lane, EXPERTS) == sec, gates, 0.0), axis=-1, keepdims=True)
        gout = (combine * gs.astype(f32)).astype(bf16)
        for f in range(NF):
            cols = slice(f * FC, (f + 1) * FC)
            z, slope = gelu_both(dot(a, r.up[:, cols]))
            z = z.astype(bf16)
            part = dot(z, r.down[cols, :])
            gv = (nt(gout, r.down[cols, :]) * slope).astype(bf16)
            gpart = nt(gv, r.up[:, cols])
            if f == 0:
                r.out_acc[...] = part
                r.ga_acc[...] = gpart
            else:
                r.out_acc[...] += part
                r.ga_acc[...] += gpart
            r.eg[0, :, cols] += tn(a, gv)
            r.eg[1, :, cols] += tn(gout, z)
        r.slot_out[j] = r.ga_acc[...].astype(bf16)
        weighted = combine * r.out_acc[...].astype(bf16).astype(f32)
        q = jnp.sum(gs.astype(f32) * weighted, axis=-1, keepdims=True)
        q_hi = q.astype(bf16).astype(f32)
        lanes = iota((SL, 128), 1)
        q2 = jnp.where(lanes == 0, q_hi, jnp.where(lanes == 1, q - q_hi, 0.0))
        r.q_out[j] = q2.T[0:16, :].astype(bf16)
        r.gslot[j] = weighted.astype(bf16)

        @pl.when(j > 0)
        def _():
            links.copy(ga_first + j, r.slot_out.at[j], ga_in(j), there).start()
            links.copy(q_first + j, r.q_out.at[j], r.q_in.at[j], there).start()
            links.copy(w_first + j, r.gslot.at[j], w_in(j), there).start()

        return carry

    lax.fori_loop(0, NS, expert_step, 0)

    def expert_copies(j):
        there = at_section(j)
        return (
            lambda: links.copy(ga_first + j, r.slot_out.at[j], ga_in(j), there),
            lambda: links.copy(q_first + j, r.q_out.at[j], r.q_in.at[j], there),
            lambda: links.copy(w_first + j, r.gslot.at[j], w_in(j), there),
        )

    links.sent = links.sent[:-3]

    e_core = links.take(NF)
    for b in range(NF):
        cols = slice(b * FC, (b + 1) * FC)
        r.up[:, cols] = r.eg[1 - core, :, cols].astype(bf16)
        links.start(e_core + b, r.up.at[:, cols], r.e_sum.at[b], mate)

    for j in range(1, NS):
        ga, q, _ = expert_copies(j)
        ga().wait()
        q().wait()

    def mix_back(i, carry):
        rows = pl.ds(pl.multiple_of(i * RP, RP), RP)
        task = jnp.zeros((RP, 1), jnp.int32) + r.task[sec, i]
        active = (lane < TASKS * EXPERTS) & (lane // EXPERTS == task)
        ga = jnp.zeros((RP, D), f32)
        q8 = jnp.zeros((RP, 128), f32)
        for j in range(NS):
            pick = onehot(r.pos_pad[rows, j : j + 1] == slot_lane)
            ga = ga + dot(pick, r.slot_out[0] if j == 0 else ga_in(j)[...])
            q = jnp.sum(nt(pick, r.q_out[0] if j == 0 else r.q_in[j]), axis=-1, keepdims=True)
            q8 = q8 + jnp.where(active & (lax.rem(lane, EXPERTS) == section_peer(j)), q, 0.0)
        gl = (q8 - r.gates[rows, :] * jnp.sum(q8, axis=-1, keepdims=True)).astype(bf16)
        ga = ga + nt(gl, r.w_rt[...])
        r.vec[V_R : V_R + 8, :] += tn(gl, r.a4[rows, :])[0:8, :]
        xhat, scale = normed(r.h3[rows, :].astype(f32))
        r.vec[V_M : V_M + 1, :] += column_sum(ga * xhat)
        r.vec[V_M + 1 : V_M + 2, :] += column_sum(ga)
        g = r.g3[rows, :].astype(f32)
        r.g2[rows, :] = (g + norm_back(ga, xhat, scale, r.mixture_gain[...])).astype(bf16)
        return carry

    lax.fori_loop(0, IMG, mix_back, 0)

    for b in range(NF):
        cols = slice(b * FC, (b + 1) * FC)
        links.copy(e_core + b, r.up.at[:, cols], r.e_sum.at[b], mate).wait_recv()
        r.e_sum[b] = (r.eg[core, :, cols] + r.e_sum[b].astype(f32)).astype(bf16)

    half_rows = D // 2
    parts = []
    for k in range(2):
        order = list(range(bits)) if k == 0 else list(range(bits))[::-1]
        parts.append(dict(rows=pl.ds(k * half_rows, half_rows), k=k, order=order, lo=0, n=NF, kept=[]))

    def chips_start(step):
        for part in parts:
            b = part["order"][step]
            v = bit_of(b)
            number = links.take()
            if part["n"] > 1:
                half = part["n"] // 2
                keep = part["lo"] + v * half
                send = part["lo"] + (1 - v) * half
            else:
                half = 1
                keep = send = part["lo"]
            land = (r.e_land, r.e_land2)[part["k"]].at[pl.ds(step + (step > 0), half)]
            made = links.start(number, r.e_sum.at[pl.ds(send, half), part["rows"]], land, at_chip(b))
            part["now"] = (made, keep, half, part["n"] > 1)
            part["made"] = made

    def chips_end(step):
        for part in parts:
            made, keep, half, halved = part["now"]
            made.wait_recv()
            if not halved:
                made.wait_send()
                links.forget(made)
            for b in range(half):
                mine = r.e_sum[keep + b, part["rows"], :].astype(f32)
                other = (r.e_land, r.e_land2)[part["k"]][step + (step > 0) + b].astype(f32)
                r.e_sum[keep + b, part["rows"], :] = (mine + other).astype(bf16)
            part["lo"], part["n"] = keep, half
            if halved:
                part["kept"].append((part["order"][step], half))

    def gather_first():
        for part in parts:
            part["at"] = part["lo"]
            for b in range(part["n"]):
                r.e_all[core, part["lo"] + b, part["rows"], :] = r.e_sum[part["lo"] + b, part["rows"], :]

    def gather_start():
        for part in parts:
            if not part["kept"]:
                part["now"] = None
                continue
            b, half = part["kept"].pop()
            number = links.take()
            here = r.e_all.at[core, pl.ds(part["at"], half), part["rows"]]
            made = links.start(number, here, here, at_chip(b))
            v = bit_of(b)
            part["now"] = (number, b, part["at"] + (1 - 2 * v) * half, half)
            part["at"] = part["at"] - v * half

    def gather_end():
        for part in parts:
            if part["now"] is None:
                continue
            number, b, first, half = part["now"]
            there = r.e_all.at[core, pl.ds(first, half), part["rows"]]
            links.copy(number, there, there, at_chip(b)).wait_recv()

    class Summed:
        def __init__(self, buffers):
            self.b = buffers

        def send_core(self):
            self.core_number = links.take()
            self.made = links.start(self.core_number, self.b.full.at[:, 1 - core], self.b.pair, mate)

        def send_section(self):
            b = self.b
            self.made.wait()
            links.forget(self.made)
            for p in range(NS):
                b.pair[p] = (b.full[p, core].astype(f32) + b.pair[p].astype(f32)).astype(bf16)
            self.numbers = [links.take() for _ in range(1, NS)]
            for j in range(1, NS):
                links.start(self.numbers[j - 1], b.pair.at[section_peer(j)], b.sec.at[j - 1], at_section(j))

        def section_sum(self):
            b = self.b
            for j in range(1, NS):
                links.copy(self.numbers[j - 1], b.sec.at[j - 1], b.sec.at[j - 1], at_section(j)).wait_recv()
            total = b.pair[sec].astype(f32)
            for j in range(1, NS):
                total = total + b.sec[j - 1].astype(f32)
            for k in range(2):
                b.fin[core, k] = self.half(total, k).astype(bf16)

        def half(self, v, k):
            if self.b.by_rows:
                h = v.shape[0] // 2
                return v[k * h : (k + 1) * h, :]
            h = v.shape[1] // 2
            return v[:, k * h : (k + 1) * h]

        def chip_start(self, step):
            self.now = []
            for k in range(2):
                bit = step if k == 0 else bits - 1 - step
                self.now.append(links.start(links.take(), self.b.fin.at[core, k], self.b.land.at[step, k], at_chip(bit)))

        def chip_end(self, step):
            for k in range(2):
                self.now[k].wait()
                links.forget(self.now[k])
                mine = self.b.fin[core, k].astype(f32)
                self.b.fin[core, k] = (mine + self.b.land[step, k].astype(f32)).astype(bf16)

        def pair_start(self):
            self.last = links.take()
            here = self.b.fin.at[core]
            links.start(self.last, here, here, mate)

        def pair_end(self):
            there = self.b.fin.at[1 - core]
            links.copy(self.last, there, there, mate).wait_recv()

    def by_section_rows(full, cols, value):
        n = D // NS // 2
        for p in range(NS):
            for c in range(2):
                full[p, c, :, cols] = value[(2 * p + c) * n : (2 * p + c + 1) * n, :].astype(bf16)

    def attention_grads(full, g_in, qkv_s, ctx_s):
        for f in range(3):
            cols = slice(f * D, (f + 1) * D)
            by_section_rows(full, cols, tn(r.a_s[...], qkv_s[:, cols]))
        by_section_rows(full, slice(3 * D, 4 * D), tn(ctx_s[...], g_in[...]))

    sum_a2, sum_du, sum_dd, sum_a1 = (Summed(b) for b in (r.t_a2, r.t_du, r.t_dd, r.t_a1))
    out_copies = []

    def send_out(src, dst):
        c = pltpu.make_async_copy(src, dst, r.out_sems.at[len(out_copies)])
        c.start()
        out_copies.append(c)

    if bits > 0:
        chips_start(0)
    attend_back(r.h2, r.g2, r.g1, att2, r.w_p2, r.w_o2, r.qkv2, r.p2, r.ctx2, V_A2)
    if bits > 0:
        chips_end(0)
    if bits > 1:
        chips_start(1)
    attention_grads(r.t_a2.full, r.g2, r.qkv2, r.ctx2)
    sum_a2.send_core()

    def dense_back(i, carry):
        rows = pl.ds(pl.multiple_of(i * HR, HR), HR)
        g = r.g1[rows, :]
        gf = g.astype(f32)
        xhat, scale = normed(r.h1[rows, :].astype(f32))
        r.a_s[rows, :] = (xhat * r.dense_gain[...] + r.dense_shift[...]).astype(bf16)
        ga = jnp.zeros((HR, D), f32)
        for f in range(NF):
            cols = slice(f * FC, (f + 1) * FC)
            gu = (nt(g, r.w_dn[cols, :]) * r.slope[rows, cols].astype(f32)).astype(bf16)
            r.slope[rows, cols] = gu
            r.vec[V_HB + f : V_HB + f + 1, :] += column_sum(gu.astype(f32))
            ga = ga + nt(gu, r.w_up[:, cols])
        r.vec[V_D : V_D + 1, :] += column_sum(ga * xhat)
        r.vec[V_D + 1 : V_D + 2, :] += column_sum(ga)
        r.vec[V_D + 2 : V_D + 3, :] += column_sum(gf)
        r.g0[rows, :] = (gf + norm_back(ga, xhat, scale, r.dense_gain[...])).astype(bf16)
        return carry

    lax.fori_loop(0, 2, dense_back, 0)
    sum_a2.send_section()
    for step in range(1, bits):
        if step > 1:
            chips_start(step)
        chips_end(step)
    gather_first()
    gather_start()

    for f in range(NF):
        cols = slice(f * FC, (f + 1) * FC)
        by_section_rows(r.t_du.full, cols, tn(r.a_s[...], r.slope[:, cols]))
    sum_du.send_core()
    for f in range(NF):
        cols = slice(f * FC, (f + 1) * FC)
        value = tn(r.g1[...], r.z[:, cols])
        n = D // 2
        for c in range(2):
            r.t_dd.full[f, c] = value[c * n : (c + 1) * n, :].astype(bf16)
    sum_dd.send_core()
    sum_a2.section_sum()
    sum_du.send_section()
    gather_end()
    gather_start()

    for j in range(1, NS):
        expert_copies(j)[2]().wait()

    def block_out(i, carry):
        rows = pl.ds(pl.multiple_of(i * RP, RP), RP)
        total = r.h3[rows, :].astype(f32)
        for j in range(NS):
            pick = onehot(r.pos_pad[rows, j : j + 1] == slot_lane)
            total = total + dot(pick, r.gslot[0] if j == 0 else w_in(j)[...])
        r.a4[rows, :] = total.astype(bf16)
        return carry

    lax.fori_loop(0, IMG, block_out, 0)
    send_out(r.a4, r.o_block)
    sum_dd.send_section()
    sum_du.section_sum()

    attend_back(r.h0, r.g0, r.g3, att1, r.w_p1, r.w_o1, r.qkv1, r.p1, r.ctx1, V_A1)
    send_out(r.g3, r.o_grad)
    sum_dd.section_sum()
    attention_grads(r.t_a1.full, r.g0, r.qkv1, r.ctx1)
    sum_a1.send_core()

    vec_core = links.take()
    made = links.start(vec_core, r.vec, r.vec_land.at[0], mate)
    gather_end()
    while any(part["kept"] for part in parts):
        gather_start()
        gather_end()
    e_last = links.take()
    here = r.e_all.at[core]
    links.start(e_last, here, here, mate)
    sum_a1.send_section()
    made.wait()
    links.forget(made)
    r.vec[...] += r.vec_land[0]
    vec_numbers = [links.take() for _ in range(1, NS)]
    vec_made = [links.start(vec_numbers[j - 1], r.vec, r.vec_land.at[j], at_section(j)) for j in range(1, NS)]
    early = (sum_a2, sum_du, sum_dd)
    for step in range(bits):
        for s in early:
            s.chip_start(step)
        for s in early:
            s.chip_end(step)
    for s in early:
        s.pair_start()
    for made in vec_made:
        made.wait()
        links.forget(made)
    r.vec[...] += r.vec_land[1] + r.vec_land[2] + r.vec_land[3]
    sum_a1.section_sum()
    for step in range(bits):
        sum_a1.chip_start(step)
        made = links.start(links.take(), r.vec, r.vec_land.at[NS + step], at_chip(step))
        sum_a1.chip_end(step)
        made.wait()
        links.forget(made)
        r.vec[...] += r.vec_land[NS + step]
    sum_a1.pair_start()
    send_out(r.vec, r.o_vec)
    there = r.e_all.at[1 - core]
    links.copy(e_last, there, there, mate).wait_recv()
    send_out(r.e_all, r.o_expert)
    for s, dst in ((sum_a2, r.o_a2), (sum_du, r.o_du), (sum_dd, r.o_dd), (sum_a1, r.o_a1)):
        s.pair_end()
        send_out(s.b.fin, dst)
    for made in links.sent:
        made.wait_send()
    for c in out_copies:
        c.wait()


class Bag:
    def __init__(self, **members):
        self.__dict__.update(members)


VECTORS = (
    "first_gain",
    "first_shift",
    "first_bias",
    "dense_gain",
    "dense_shift",
    "hidden_bias",
    "dense_bias",
    "second_gain",
    "second_shift",
    "second_bias",
    "mixture_gain",
    "mixture_shift",
)
HBM_IN = ("patches", "cotangent", "s_p1", "s_o1", "s_up", "s_dn", "s_p2", "s_o2", "s_rt", "expert_up", "expert_down")


def run_blocks(bits, arrays):
    R, D = arrays["patches"].shape[1:]
    FF = arrays["expert_up"].shape[2]
    IMG = R // PATCHES
    RT = IMG * RP
    n = D // 8
    vm = pltpu.VMEM
    scratch = dict(
        pool=vm((max(4 * R, 6 * SL), D), bf16),
        chosen=vm((16, R), f32),
        pos_pad=vm((RT, 16), f32),
        pos_raw=vm((R, 16), f32),
        w_p1=vm((D, 3 * D), bf16),
        w_o1=vm((D, D), bf16),
        w_up=vm((D, FF), bf16),
        w_dn=vm((FF, D), bf16),
        w_p2=vm((D, 3 * D), bf16),
        w_o2=vm((D, D), bf16),
        w_rt=vm((D, 128), bf16),
        up=vm((D, FF), bf16),
        down=vm((FF, D), bf16),
        h0=vm((RT, D), bf16),
        h1=vm((RT, D), bf16),
        h2=vm((RT, D), bf16),
        h3=vm((RT, D), bf16),
        g0=vm((RT, D), bf16),
        g1=vm((RT, D), bf16),
        g2=vm((RT, D), bf16),
        g3=vm((RT, D), bf16),
        a_s=vm((RT, D), bf16),
        a4=vm((RT, D), bf16),
        qkv1=vm((RT, 3 * D), bf16),
        qkv2=vm((RT, 3 * D), bf16),
        p1=vm((IMG * HEADS, RP, RP), bf16),
        p2=vm((IMG * HEADS, RP, RP), bf16),
        ctx1=vm((RT, D), bf16),
        ctx2=vm((RT, D), bf16),
        z=vm((RT, FF), bf16),
        slope=vm((RT, FF), bf16),
        gates=vm((RT, 128), f32),
        slot_out=vm((4, SL, D), bf16),
        slot_in=vm((4, SL, D), bf16),
        gslot=vm((4, SL, D), bf16),
        tslot=vm((4, SL, 128), bf16),
        q_out=vm((4, 16, SL), bf16),
        q_in=vm((4, 16, SL), bf16),
        out_acc=vm((SL, D), f32),
        ga_acc=vm((SL, D), f32),
        eg=vm((2, D, FF), f32),
        e_sum=vm((4, D, D), bf16),
        e_land=vm((bits + 1, D // 2, D), bf16),
        e_land2=vm((bits + 1, D // 2, D), bf16),
        e_all=vm((2, 4, D, D), bf16),
        vec=vm((VROWS, D), f32),
        vec_land=vm((4 + max(bits, 1), VROWS, D), f32),
        send=pltpu.SemaphoreType.DMA((NSEM,)),
        recv=pltpu.SemaphoreType.DMA((NSEM,)),
        local=pltpu.SemaphoreType.DMA((16,)),
        out_sems=pltpu.SemaphoreType.DMA((8,)),
    )
    sums = dict(t_a2=False, t_du=False, t_dd=True, t_a1=False)
    fin = {}
    for name, by_rows in sums.items():
        rows, cols = (D // 2, D) if by_rows else (n, FF)
        halved = (rows // 2, cols) if by_rows else (rows, cols // 2)
        if name in ("t_a2", "t_dd"):
            scratch[name + ".full"] = vm((4, 2, rows, cols), bf16)
        scratch[name + ".pair"] = vm((4, rows, cols), bf16)
        scratch[name + ".sec"] = vm((3, rows, cols), bf16)
        scratch[name + ".fin"] = vm((2, 2) + halved, bf16)
        scratch[name + ".land"] = vm((max(bits, 1), 2) + halved, bf16)
        fin[name] = jax.ShapeDtypeStruct((2, 2) + halved, bf16)
    outs = dict(
        o_block=jax.ShapeDtypeStruct((RT, D), bf16),
        o_grad=jax.ShapeDtypeStruct((RT, D), bf16),
        o_expert=jax.ShapeDtypeStruct((2, 4, D, D), bf16),
        o_a2=fin["t_a2"],
        o_du=fin["t_du"],
        o_dd=fin["t_dd"],
        o_a1=fin["t_a1"],
        o_vec=jax.ShapeDtypeStruct((VROWS, D), f32),
    )
    ins = list(arrays)
    names = ins + list(outs) + list(scratch)
    spaces = {name: pl.BlockSpec(memory_space=pl.ANY) for name in HBM_IN}
    spaces["task"] = pl.BlockSpec(memory_space=pltpu.SMEM)

    def body(*refs):
        members = {}
        for name, ref in zip(names, refs, strict=True):
            if "." in name:
                outer, inner = name.split(".")
                members.setdefault(outer, Bag(by_rows=sums[outer])).__dict__[inner] = ref
            else:
                members[name] = ref
        for name in ("t_du", "t_a1"):
            members[name].full = members["t_a2"].full
        block_kernel(bits, Bag(**members))

    return pl.pallas_call(
        body,
        out_shape=list(outs.values()),
        in_specs=[spaces.get(name, pl.BlockSpec(memory_space=pltpu.VMEM)) for name in ins],
        out_specs=[pl.BlockSpec(memory_space=pl.ANY)] * len(outs),
        scratch_shapes=list(scratch.values()),
        compiler_params=pltpu.CompilerParams(
            collective_id=0, has_side_effects=True, vmem_limit_bytes=64 * 2**20 - 2**18
        ),
        name="blocks",
    )(*arrays.values())


def finish_kernel(block, grad, expert, a2, du, dd, a1, vec, *outs):
    (
        o_block, o_grad, g1, s1, p1, o1, b1, gd, sd, up, hb, dn, db, g2, s2, p2, o2, b2, gm, sm, rt, eup, edn,
    ) = outs
    D = block.shape[1]
    R = o_block.shape[1]
    sec = lax.axis_index("section")
    row, col = iota((R, RP), 0), iota((R, RP), 1)
    for src, dst in ((block, o_block), (grad, o_grad)):
        total = jnp.zeros((R, D), f32)
        for i in range(R // PATCHES):
            pick = onehot((row - i * PATCHES == col) & (col < PATCHES))
            total = total + dot(pick, src[i * RP : (i + 1) * RP, :])
        dst[0] = total.astype(bf16)
    n = D // 8
    for src, dst_p, dst_o in ((a1, p1, o1), (a2, p2, o2)):
        for c in range(2):
            rows = slice(c * n, (c + 1) * n)
            dst_p[rows, 0 : 2 * D] = src[c, 0].astype(f32)
            dst_p[rows, 2 * D : 3 * D] = src[c, 1, :, 0:D].astype(f32)
            dst_o[rows, :] = src[c, 1, :, D : 2 * D].astype(f32)
    for c in range(2):
        for k in range(2):
            up[c * n : (c + 1) * n, k * 2 * D : (k + 1) * 2 * D] = du[c, k].astype(f32)
    down_t = jnp.concatenate([dd[0, 0], dd[0, 1], dd[1, 0], dd[1, 1]], axis=0)
    dn[...] = down_t.astype(f32).T
    for b in range(4):
        eup[0, :, b * D : (b + 1) * D] = expert[0, b].astype(f32)
        edn[0, b * D : (b + 1) * D, :] = expert[1, b].astype(f32).T
    q = D // 4
    mine = jnp.where(iota((D, q), 0) == iota((D, q), 1) + sec * q, 1.0, 0.0)
    cut = jnp.dot(vec[...], mine, precision=lax.Precision.HIGHEST, preferred_element_type=f32)
    for dst, at in (
        (g1, V_A1), (s1, V_A1 + 1), (b1, V_A1 + 2), (gd, V_D), (sd, V_D + 1), (db, V_D + 2),
        (g2, V_A2), (s2, V_A2 + 1), (b2, V_A2 + 2), (gm, V_M), (sm, V_M + 1),
    ):
        dst[...] = cut[at : at + 1, :]
    rt[...] = cut[V_R : V_R + 8, :]
    hb[...] = vec[pl.ds(V_HB + sec, 1), :]


def finish(parts, shape):
    R, D, FF = shape
    q = D // 4
    s = lambda *dims: jax.ShapeDtypeStruct(dims, f32)
    outs = [
        jax.ShapeDtypeStruct((1, R, D), bf16), jax.ShapeDtypeStruct((1, R, D), bf16),
        s(1, q), s(1, q), s(q, 3 * D), s(q, D), s(1, q),
        s(1, q), s(1, q), s(q, FF), s(1, FF // 4), s(FF // 4, D), s(1, q),
        s(1, q), s(1, q), s(q, 3 * D), s(q, D), s(1, q),
        s(1, q), s(1, q), s(8, q), s(1, D, FF), s(1, FF, D),
    ]
    return pl.pallas_call(
        finish_kernel,
        out_shape=outs,
        in_specs=[pl.BlockSpec(memory_space=pltpu.VMEM)] * 8,
        out_specs=[pl.BlockSpec(memory_space=pltpu.VMEM)] * len(outs),
        compiler_params=pltpu.CompilerParams(vmem_limit_bytes=48 * 2**20),
        name="finish",
    )(*parts)


def local(
    patches_in, cotangent, task_ids, routes, keep_mask,
    first_gain, first_shift, first_proj, first_out, first_bias,
    dense_gain, dense_shift, dense_up, hidden_bias, dense_down, dense_bias,
    second_gain, second_shift, second_proj, second_out, second_bias,
    mixture_gain, mixture_shift, router, expert_up, expert_down,
):
    bits = (lax.axis_size("wide") // 2).bit_length() - 1
    line = lambda v: v.reshape(1, -1)
    arrays = dict(
        patches=patches_in,
        cotangent=cotangent,
        task=task_ids,
        routes=jnp.transpose(routes, (0, 2, 1)),
        keep=jnp.transpose(keep_mask, (0, 2, 1)),
        s_p1=first_proj,
        s_o1=first_out,
        s_up=dense_up,
        s_dn=dense_down,
        s_p2=second_proj,
        s_o2=second_out,
        s_rt=jnp.pad(router, ((0, 0), (0, 128 - router.shape[1]))),
        expert_up=expert_up,
        expert_down=expert_down,
        first_gain=line(first_gain),
        first_shift=line(first_shift),
        first_bias=line(first_bias),
        dense_gain=line(dense_gain),
        dense_shift=line(dense_shift),
        hidden_bias=line(hidden_bias),
        dense_bias=line(dense_bias),
        second_gain=line(second_gain),
        second_shift=line(second_shift),
        second_bias=line(second_bias),
        mixture_gain=line(mixture_gain),
        mixture_shift=line(mixture_shift),
    )
    parts = run_blocks(bits, arrays)
    R, D = patches_in.shape[1:]
    outs = list(finish(parts, (R, D, expert_up.shape[2])))
    for at in (2, 3, 6, 7, 8, 10, 12, 13, 14, 17, 18, 19):
        outs[at] = outs[at].reshape(-1)
    outs[20] = outs[20].T
    return tuple(outs)


def solution(mesh):
    rows, vec, mat = P(None, "wide", None), P(), P("section", None)
    cube = P("section", None, None)
    in_specs = (
        rows, rows, P(None, "wide"), rows, rows,
        vec, vec, mat, mat, vec,
        vec, vec, mat, vec, mat, vec,
        vec, vec, mat, mat, vec,
        vec, vec, mat, cube, cube,
    )
    cut, moved = P("section"), P("section", "wide", None)
    out_specs = (
        moved, moved,
        cut, cut, mat, mat, cut,
        cut, cut, mat, cut, mat, cut,
        cut, cut, mat, mat, cut,
        cut, cut, mat, cube, cube,
    )
    return jax.shard_map(local, mesh=mesh, in_specs=in_specs, out_specs=out_specs, check_vma=False)
```

time: 3410 us -> 228 us (0.07)
  waiting for transfers between devices: 1220 us -> 0 us
  local copies, waits for them, and re-layouts: 819 us -> 24.9 us
  blocking collectives: 371 us -> 0 us
  other arithmetic: 289 us -> 0.6 us
  starting transfers between devices: 281 us -> 0 us
  loops' own time: 280 us -> 0 us
  Pallas kernels: 0 us -> 201 us
  matrix products: 123 us -> 0 us
    ppermute x14 -> x0, waiting for transfers between devices: 989 us -> none  [passed_along(): return lax.ppermute(block, axis, route)]
    psum x1 -> x0, blocking collectives: 371 us -> none  [local(): summed = lax.psum(packed, 'wide')]
    unnamed x109 -> x17, local copies, waits for them, and re-layouts: 307 us -> 9.25 us
    another operation x16 -> x0, loops' own time: 280 us -> none  [the longest x7 160 us: backward_step(): lax.switch(jnp.where(working, section_index, 4), backward_branches, store...]
    ppermute x14 -> x0, starting transfers between devices: 270 us -> none  [passed_along(): return lax.ppermute(block, axis, route)]
    all_to_all x2 -> x0, waiting for transfers between devices: 225 us -> none  [the longest x1 121 us: local(): lax.all_to_all(summed.astype(jnp.bfloat16), 'section', split_axis=0, conc...]
    pallas_call x0 -> x2, Pallas kernels: none -> 201 us  [the longest x1 196 us: run_blocks(): pl.pallas_call(body, out_shape=list(outs.values()), in_specs=[spaces.get(...]
    another operation x45 -> x0, local copies, waits for them, and re-layouts: 151 us -> none  [the longest x4 111 us: local(): jnp.stack(rows_out, axis=0)]
  transfers between devices with their start and end apart: 18 -> 0, of which waited for: 16 -> 0; matrix products, arithmetic and copies ran while one was open for 4% -> 0% of each run, Pallas kernels for 0% -> 0%
where the time goes in v1:
time: 228 us; the launch traced here: 227 us
  Pallas kernels  201 us (88%)
  local copies, waits for them, and re-layouts  24.9 us (11%)
    pallas_call x1, Pallas kernels, run_blocks(): pl.pallas_call(body, out_shape=list(outs.values()), in_specs=[spaces.get(...  196 us
    reshape x12, local copies, waits for them, and re-layouts, local(): line = lambda v: v.reshape(1, -1)  15 us
    unnamed x17, local copies, waits for them, and re-layouts  9.25 us
    pallas_call x1, Pallas kernels, finish(): pl.pallas_call(finish_kernel, out_shape=outs, in_specs=[pl.BlockSpec(memo...  5.27 us

profile of v1, /device:TPU:0, one launch (start us, length us, event | category | flops | bytes accessed | tf_op | source)
XLA Modules:
  0.0 227.4 jit_solution(11328934596231809358)
XLA Ops:
  0.7 1.2 reshape.118.refs_14_
  1.9 1.2 reshape.119.refs_15_
  3.1 1.2 reshape.120.refs_16_
  4.4 1.2 reshape.121.refs_17_
  5.6 1.2 reshape.122.refs_18_
  6.9 1.2 reshape.124.refs_20_
  8.1 1.2 reshape.125.refs_21_
  9.4 1.2 reshape.126.refs_22_
  10.6 1.2 reshape.127.refs_23_
  11.9 1.2 reshape.128.refs_24_
  13.1 1.2 reshape.129.refs_25_
  14.4 1.3 reshape.123.refs_19_
  15.6 0.8 copy.49
  16.4 0.6 pad.4.refs_11_
  17.1 196.0 %blocks.1 = (bf16[832,384]{1,0:T(8,128)(2,1)}, bf16[832,384]{1,0:T(8,128)(2,1)}, bf16[2,4,384,384]{3,2,1,0:T(8,128)(2,1)}, bf16[2,2,48,768]{3,2,1,0:T(8,128)(2,1...) custom-call(bf16[4,784,384]{2,1,0:T(8,128)(2,1)} %refs_0_.1, ...), custom_call_target="tpu_custom_call" | custom-call | tf_op jit(solution)/shard_map/blocks/pallas_call | solution.py:911
  213.0 0.0 copy-start
  213.1 1.7 copy-done
  214.7 0.0 copy-start.1
  214.7 1.1 copy-done.1
  215.8 0.0 copy-start.2
  215.8 1.1 copy-done.2
  216.9 0.0 copy-start.3
  216.9 1.0 copy-done.3
  217.8 0.0 copy-start.4
  217.8 1.0 copy-done.4
  218.8 0.0 copy-start.5
  218.8 1.0 copy-done.5
  219.8 0.0 copy-start.6
  219.8 1.0 copy-done.6
  220.7 0.0 copy-start.7
  220.7 0.8 copy-done.7
  221.5 5.3 %finish.1 = (bf16[1,784,384]{2,1,0:T(8,128)(2,1)}, bf16[1,784,384]{2,1,0:T(8,128)(2,1)}, f32[1,96]{1,0:T(1,128)}, f32[1,96]{1,0:T(1,128)}, f32[96,1152]{1,0:T(8,...) custom-call(bf16[832,384]{1,0:T(8,128)(2,1)S(1)} %copy-done.1, ...), custom_call_target="tpu_custom_call" | custom-call | tf_op jit(solution)/shard_map/finish/pallas_call | solution.py:976
  226.8 0.6 reduce
Async XLA Ops:
  213.0 1.7 copy-start
  214.7 1.1 copy-start.1
  215.8 1.1 copy-start.2
  216.9 1.0 copy-start.3
  217.8 1.0 copy-start.4
  218.8 1.0 copy-start.5
  219.8 1.0 copy-start.6
  220.7 0.8 copy-start.7
